TPU v7x, 32 devices: a whole 2x2x4 slice. The times are simulated.
32 devices in a mesh: dp: 8 (over y, x, core), mp: 4 (over z).
Axes of the slice: x: 2, y: 2, z: 4, core: 2. Of those that a mesh axis runs over, the one named last changes fastest.
Arguments:
- tokens: bfloat16 [4096, 768], P(('dp', 'mp'))
- cotangent: bfloat16 [4096, 768], P(('dp', 'mp')), may hold values from -6 to 6
- seq_starts: int32 [8, 8], P('dp'), may hold values from 0 to 511, as said below
- attn_weight: float32 [4, 768, 768], replicated
- up_weight: float32 [768, 3072], P(None, 'mp')
- down_weight: float32 [3072, 768], P('mp')
- vec_params: float32 [4, 768], replicated
- attn_stats: float32 [4, 2, 768], replicated
- ffn_narrow_stats: float32 [2, 768], replicated
- ffn_wide_stats: float32 [2, 3072], P(None, 'mp')
- vec_moment: float32 [4, 768], replicated
Outputs:
- block_out: float32 [4096, 768], P(('dp', 'mp'))
- tokens_grad: float32 [4096, 768], P(('dp', 'mp'))
- attn_grad: float32 [4, 768, 768], P(None, 'mp')
- attn_row_stats: float32 [4, 768], P(None, 'mp')
- attn_col_stats: float32 [4, 768], replicated
- attn_new: float32 [4, 768, 768], P(None, 'mp')
- attn_new_low: bfloat16 [4, 768, 768], P(None, 'mp')
- up_grad: float32 [768, 3072], P(None, 'mp')
- down_grad: float32 [3072, 768], P('mp')
- ffn_narrow_new: float32 [2, 768], replicated
- ffn_wide_new: float32 [2, 3072], P(None, 'mp')
- up_new: float32 [768, 3072], P(None, 'mp')
- down_new: float32 [3072, 768], P('mp')
- up_new_low: bfloat16 [768, 3072], P(None, 'mp')
- down_new_low: bfloat16 [3072, 768], P('mp')
- vec_grad: float32 [4, 768], replicated
- vec_moment_new: float32 [4, 768], replicated
- vec_new: float32 [4, 768], replicated
Inputs may be any that keep to these rules, and one draw needn't show every extreme that they name: `seq_starts`: each row rises strictly from 0; its sequences fill the pack's 512 tokens. One sequence of each pack, at a place drawn from the seed, is at least 386 tokens long; the others have 1 to 18 tokens. In one pack, drawn from the seed, the last sequence is a single token.
All inputs are finite; a program needn't handle non-finite values.
Results may differ from a plain program's by a relative error of at most 0.0094.
Values may be sent and summed in bfloat16 or wider, within the bound.
No kernel may reach another device: no remote copies, remote signals or barrier semaphores. Data moves between devices by JAX's collectives and lax.ppermute only.
A program may use at most 192 MiB of HBM per device.

v0:
```python
import functools
import math

import jax
import jax.numpy as jnp
from jax import lax
from jax.experimental import pallas as pl
from jax.experimental.pallas import tpu as pltpu
from jax.sharding import PartitionSpec as P

HEADS = 12
STEP = 10

norm_eps = 1e-05
tiny_square = 1e-30
learn_rate = 0.3
clip_limit = 1.0
decay = 1.0 - float(STEP) ** (-0.8)

f32 = jnp.float32
bf16 = jnp.bfloat16

NN = (((1,), (0,)), ((), ()))
NT = (((1,), (1,)), ((), ()))
TN = (((0,), (0,)), ((), ()))


def mm(a, b, dims=NN):
    return lax.dot_general(a, b, dims, preferred_element_type=f32)


def params(mib):
    return pltpu.CompilerParams(vmem_limit_bytes=mib * 1024 * 1024)


def sds(shape, dtype):
    return jax.ShapeDtypeStruct(shape, dtype)


def in_hbm(array):
    return pltpu.with_memory_space_constraint(array, pltpu.HBM)


def in_vmem(array):
    return pltpu.with_memory_space_constraint(array, pltpu.VMEM)


def all_vmem(arrays):
    return [in_vmem(array) for array in arrays]


def near(shape, dtype):
    return pltpu.VMEM(shape, dtype)


NO_COST = pl.CostEstimate(flops=0, bytes_accessed=0, transcendentals=0)


def holding(kernel, count, held):
    def body(*refs):
        for ref in refs[count : count + held]:
            pltpu.touch(ref)
        kernel(*refs[:count], *refs[count + held :])

    return body


STAGED = 8
VEC_ROWS = 16
TOKEN_STEPS = (0, -2, -1, -3)
BRANCH_STEPS = (0, 1, 2, 3)
BACK_STEPS = (0, 2, 1, 3)
FIRST_STEPS = (0, 1, 2, 3)
MIX_STEPS = (0, 2, 1, 3)
SHARE_STEPS = (0, -1, -2, -3)


def target(rank, step, ranks):
    return rank ^ -step if step <= 0 else (rank + step) % ranks


def source(rank, step, ranks):
    return rank ^ -step if step <= 0 else (rank + ranks - step) % ranks


def rank_rows(rank, rows):
    return pl.ds(pl.multiple_of(rank * rows, rows), rows)


def half_rows(count, mine):
    rows = count // 2
    side = lax.rem(lax.axis_index("dp"), 2) if lax.axis_size("dp") == STAGED else 0
    return pl.ds(pl.multiple_of((side if mine else 1 - side) * rows, rows), rows)


def write_halves(total, keep, send):
    rows = total.shape[0] // 2
    keep[...] = total[half_rows(total.shape[0], True), :]
    send[0:rows, :] = total[half_rows(total.shape[0], False), :].astype(send.dtype)


def read_halves(mine, other, total):
    total[half_rows(total.shape[0], True), :] = mine[...].astype(total.dtype)
    total[half_rows(total.shape[0], False), :] = other[...].astype(total.dtype)


def two_parts(values):
    high = values.astype(bf16).astype(f32)
    low = (values - high).astype(bf16).astype(f32)
    both = jnp.concatenate([high, low], axis=0)
    return high + low, jnp.concatenate([both, jnp.zeros_like(both)], axis=0).astype(bf16)


def joined(block):
    block = block.astype(f32)
    return block[0:4, :] + block[4:8, :]


def add_vec(vec, block, vec_out, send=None):
    held, packed = two_parts(vec[0:4, :] + joined(block))
    vec_out[0:4, :] = held
    vec_out[4:8, :] = jnp.zeros_like(held)
    if send is not None:
        send[...] = packed


def fold_first_kernel(keep, received, *refs):
    send_a, send_b = refs[-2:]
    rows = keep.shape[0] // 2
    send_a[0:rows, :] = (keep[0:rows, :] + received[0:rows, :].astype(f32)).astype(bf16)
    send_b[...] = (keep[rows : 2 * rows, :] + received[rows : 2 * rows, :].astype(f32)).astype(bf16)
    if len(refs) > 2:
        add_vec(refs[0], received[2 * rows :, :], refs[1], send_a.at[rows:, :])


def fold_second_kernel(own_a, got_a, own_b, got_b, *refs):
    send_a, send_b = refs[-2:]
    rows = own_b.shape[0]
    send_a[0:rows, :] = (own_a[0:rows, :].astype(f32) + got_a[0:rows, :].astype(f32)).astype(bf16)
    send_b[...] = (own_b[...].astype(f32) + got_b[...].astype(f32)).astype(bf16)
    if len(refs) > 2:
        add_vec(refs[0], got_a[rows:, :], refs[1], send_a.at[rows:, :])


def fold_last_kernel(own_a, got_a, own_b, got_b, *refs):
    total = refs[-1]
    rows = own_b.shape[0]
    total[0:rows, :] = (own_a[0:rows, :].astype(f32) + got_a[0:rows, :].astype(f32)).astype(bf16)
    total[rows:, :] = (own_b[...].astype(f32) + got_b[...].astype(f32)).astype(bf16)
    if len(refs) > 1:
        add_vec(refs[0], got_a[rows:, :], refs[1])


def fold_call(kernel, name, inputs, vec, outs):
    width = inputs[0].shape[1]
    extra_in, extra_out = ([in_vmem(vec)], [near((8, width), f32)]) if vec is not None else ([], [])
    return pl.pallas_call(
        kernel,
        out_shape=extra_out + [near((rows, width), bf16) for rows in outs],
        compiler_params=params(8),
        cost_estimate=NO_COST,
        name=name,
    )(in_vmem(inputs[0]), *inputs[1:], *extra_in)


def fold_first(keep, received, vec=None):
    rows = keep.shape[0] // 2
    return fold_call(
        fold_first_kernel, "fold_first", (keep, received), vec, (rows if vec is None else rows + VEC_ROWS, rows)
    )


def fold_second(own_a, got_a, own_b, got_b, vec=None):
    return fold_call(
        fold_second_kernel, "fold_second", (own_a, got_a, own_b, got_b), vec, (own_a.shape[0], own_b.shape[0])
    )


def fold_last(own_a, got_a, own_b, got_b, vec=None):
    return fold_call(fold_last_kernel, "fold_last", (own_a, got_a, own_b, got_b), vec, (2 * own_b.shape[0],))


def fold_feed_kernel(*refs):
    own, got, (send_a, send_b) = refs[0:4], refs[4:8], refs[8:]
    rows = own[0].shape[0]
    for n, (block, other) in enumerate(zip(own, got)):
        send = (send_a, send_b)[n % 2]
        place = n // 2 * rows
        send[place : place + rows, :] = (block[...].astype(f32) + other[...].astype(f32)).astype(bf16)


def fold_feed(own, got):
    rows, width = own[0].shape
    return pl.pallas_call(
        fold_feed_kernel,
        out_shape=[near((2 * rows, width), bf16)] * 2,
        compiler_params=params(8),
        cost_estimate=NO_COST,
        name="fold_feed",
    )(*all_vmem(own), *got)


def fold_feed_last_kernel(own_a, got_a, own_b, got_b, total):
    rows = own_a.shape[0] // 2
    for n, (block, other) in enumerate(((own_a, got_a), (own_b, got_b))):
        for part in range(2):
            here = slice(part * rows, (part + 1) * rows)
            place = (2 * part + n) * rows
            total[place : place + rows, :] = (block[here, :].astype(f32) + other[here, :].astype(f32)).astype(bf16)


def fold_feed_last(own_a, got_a, own_b, got_b):
    rows, width = own_a.shape
    return pl.pallas_call(
        fold_feed_last_kernel,
        out_shape=near((2 * rows, width), bf16),
        compiler_params=params(8),
        cost_estimate=NO_COST,
        name="fold_feed_last",
    )(in_vmem(own_a), got_a, in_vmem(own_b), got_b)


def across(block, bit):
    return lax.ppermute(block, "dp", [(i, i ^ bit) for i in range(STAGED)])


def prepare_kernel(seqs, tokens_pack, starts, attn, up, down, attn_low, up_low, down_low, mask, mask_t, squares):
    step = pl.program_id(0)

    @pl.when(step == 0)
    def _():
        squares[...] = jnp.zeros_like(squares)

    for k in range(4):
        block = attn[k]
        attn_low[k] = block.astype(bf16)
        squares[k : k + 1, :] += jnp.sum(block * block, axis=0, keepdims=True)
    for k, (source, target) in enumerate(((up, up_low), (down, down_low))):
        block = source[...]
        target[...] = block.astype(bf16)
        squares[4 + k : 5 + k, :] += jnp.sum(block * block, axis=0, keepdims=True)

    def layout(index):
        seq = jnp.zeros_like(index)
        begin = jnp.zeros_like(index)
        length = jnp.ones_like(index)
        for s in range(seqs):
            start = starts[0, s]
            finish = starts[0, s + 1] if s + 1 < seqs else tokens_pack
            inside = index >= start
            seq = jnp.where(inside, s, seq)
            begin = jnp.where(inside, start, begin)
            length = jnp.where(inside, finish - start, length)
        angle = 0.5 * math.pi * (index - begin).astype(f32) / length.astype(f32)
        return seq, jnp.cos(angle), jnp.sin(angle)

    rows = mask.shape[0]
    row = lax.broadcasted_iota(jnp.int32, (rows, 128), 0) + step * rows
    col = lax.broadcasted_iota(jnp.int32, (8, tokens_pack), 1)
    row_seq, row_cos, row_sin = (a[:, 0:1] for a in layout(row))
    col_seq, col_cos, col_sin = (a[0:1, :] for a in layout(col))
    same = row_seq == col_seq
    value = row_cos * col_cos + row_sin * col_sin
    row, col = row[:, 0:1], col[0:1, :]
    mask[...] = jnp.where(same & (col <= row), value, 0.0)
    mask_t[...] = jnp.where(same & (row <= col), value, 0.0)


def prepare(seq_starts, attn_weight, up_weight, down_weight, tokens_pack):
    steps = 8
    seqs = seq_starts.shape[1]
    heads4, width, _ = attn_weight.shape
    hidden = up_weight.shape[1]
    a_rows, u_rows, d_rows, m_rows = width // steps, width // steps, hidden // steps, tokens_pack // steps
    return pl.pallas_call(
        functools.partial(prepare_kernel, seqs, tokens_pack),
        grid=(steps,),
        in_specs=[
            pl.BlockSpec(memory_space=pltpu.SMEM),
            pl.BlockSpec((4, a_rows, width), lambda i: (0, i, 0)),
            pl.BlockSpec((u_rows, hidden), lambda i: (i, 0)),
            pl.BlockSpec((d_rows, width), lambda i: (i, 0)),
        ],
        out_specs=[
            pl.BlockSpec((4, a_rows, width), lambda i: (0, i, 0)),
            pl.BlockSpec((u_rows, hidden), lambda i: (i, 0)),
            pl.BlockSpec((d_rows, width), lambda i: (i, 0)),
            pl.BlockSpec((m_rows, tokens_pack), lambda i: (i, 0)),
            pl.BlockSpec((m_rows, tokens_pack), lambda i: (i, 0)),
            pl.BlockSpec((8, width), lambda i: (0, 0)),
        ],
        out_shape=[
            near((4, width, width), bf16),
            near((width, hidden), bf16),
            near((hidden, width), bf16),
            near((tokens_pack, tokens_pack), f32),
            near((tokens_pack, tokens_pack), f32),
            near((8, width), f32),
        ],
        compiler_params=params(24),
        cost_estimate=pl.CostEstimate(flops=10_000_000, bytes_accessed=22_000_000, transcendentals=0),
        name="prepare",
    )(seq_starts, in_hbm(attn_weight), in_hbm(up_weight), in_hbm(down_weight))


def half_lanes(width):
    return lax.broadcasted_iota(jnp.int32, (1, width), 1) < width // 2


def norm_parts(values):
    centered = values - jnp.mean(values, axis=-1, keepdims=True)
    spread = lax.rsqrt(jnp.mean(centered * centered, axis=-1, keepdims=True) + norm_eps)
    return centered * spread, spread


def norm_back(grad, unit, spread, gain):
    scaled = grad * gain
    return spread * (
        scaled
        - jnp.mean(scaled, axis=-1, keepdims=True)
        - unit * jnp.mean(scaled * unit, axis=-1, keepdims=True)
    )


def causal_blocks(tokens, size):
    return [(i, min(size, tokens - i)) for i in range(0, tokens, size)]


def forward_kernel(
    local,
    x0,
    x1,
    x2,
    x3,
    attn_low,
    up_low,
    down_low,
    mask,
    vec,
    x_all,
    query_feat,
    key_feat,
    value_low,
    mixed_low,
    inverse,
    own_sum,
    own_first,
    first_low,
    pre_act,
    hidden_low,
    part0,
    part1,
    part2,
    part3,
    branch,
):
    rank = lax.axis_index("mp")
    tokens, width = x_all.shape
    ranks = tokens // local

    for step, block in zip(TOKEN_STEPS, (x0, x1, x2, x3)):
        x_all[rank_rows(source(rank, step, ranks), local), :] = block[...]

    piece = 256
    for c in range(0, width, piece):
        cols = slice(c, c + piece)
        for which, feat in ((0, query_feat), (1, key_feat)):
            raw = mm(x_all[...], attn_low[which, :, cols])
            feat[:, cols] = jax.nn.softplus(raw).astype(bf16)
        value_low[:, cols] = mm(x_all[...], attn_low[2, :, cols]).astype(bf16)

    pair = 2 * (width // HEADS)
    first_half = half_lanes(pair)
    for c in range(0, width, pair):
        cols = slice(c, c + pair)
        keys = key_feat[:, cols]
        values = value_low[:, cols]
        zero = jnp.zeros_like(keys)
        one = jnp.ones_like(values)
        sides = (first_half, ~first_half)
        own_keys = [jnp.where(own, keys, zero) for own in sides]
        own_values = [
            jnp.concatenate([jnp.where(own, values, zero), jnp.where(own, one, zero)], axis=1) for own in sides
        ]
        for i, rows in causal_blocks(tokens, 256):
            here = slice(i, i + rows)
            upto = i + rows
            queries = query_feat[here, cols]
            allowed = mask[here, :upto]
            scores = mm(queries, jnp.concatenate([block[:upto] for block in own_keys], axis=0), NT)
            weights = (scores * jnp.concatenate([allowed, allowed], axis=1)).astype(bf16)
            both = mm(weights, jnp.concatenate([block[:upto] for block in own_values], axis=0))
            inv = 1.0 / both[:, pair:]
            inverse[here, cols] = inv
            mixed_low[here, cols] = (both[:, :pair] * inv).astype(bf16)

    for i, rows in causal_blocks(tokens, 256):
        here = slice(i, i + rows)
        summed = x_all[here, :].astype(f32) + mm(mixed_low[here, :], attn_low[3])
        branch[here, :] = summed
        unit, _ = norm_parts(summed)
        first_low[here, :] = (unit * vec[0:1, :] + vec[1:2, :]).astype(bf16)
    own_sum[...] = branch[rank_rows(rank, local), :]
    unit, _ = norm_parts(own_sum[...])
    own_first[...] = unit * vec[0:1, :] + vec[1:2, :]

    hidden_count = up_low.shape[1]
    for c in range(0, hidden_count, piece):
        cols = slice(c, c + piece)
        pre = mm(first_low[...], up_low[:, cols])
        cdf = 0.5 * (1.0 + lax.erf(pre * math.sqrt(0.5)))
        hidden_low[:, cols] = (pre * cdf).astype(bf16)
        pre_act[:, cols] = pre

    branch[...] = mm(hidden_low[...], down_low[...])
    for step, part in zip(BRANCH_STEPS, (part0, part1, part2, part3)):
        part[...] = branch[rank_rows(target(rank, step, ranks), local), :].astype(part.dtype)


def forward(blocks, attn_low, up_low, down_low, mask, vec):
    local, width = blocks[0].shape
    tokens = mask.shape[0]
    hidden = up_low.shape[1]
    return pl.pallas_call(
        functools.partial(forward_kernel, local),
        out_shape=[near((tokens, width), bf16)] * 5
        + [near((tokens, width), f32), near((local, width), f32), near((local, width), f32)]
        + [near((tokens, width), bf16), near((tokens, hidden), f32), near((tokens, hidden), bf16)]
        + [near((local, width), f32)]
        + [near((local, width), bf16)] * 3,
        scratch_shapes=[pltpu.VMEM((tokens, width), f32)],
        compiler_params=params(16),
        cost_estimate=pl.CostEstimate(flops=8_000_000_000, bytes_accessed=20_000_000, transcendentals=2_000_000),
        name="forward",
    )(*blocks, *all_vmem((attn_low, up_low, down_low, mask)), vec)


def slopes_kernel(query_feat, key_feat, mask_t, pre_act, weights_t, query_slope, key_slope, slope):
    tokens, width = query_feat.shape
    piece = 256
    for c in range(0, width, piece):
        cols = slice(c, c + piece)
        for feat, grad in ((query_feat, query_slope), (key_feat, key_slope)):
            value = feat[:, cols].astype(f32)
            small = value * (1.0 - value * (0.5 - value * (1.0 / 6.0)))
            grad[:, cols] = jnp.where(value < 0.02, small, 1.0 - jnp.exp(-value)).astype(bf16)
    for c in range(0, pre_act.shape[1], piece):
        cols = slice(c, c + piece)
        pre = pre_act[:, cols]
        cdf = 0.5 * (1.0 + lax.erf(pre * math.sqrt(0.5)))
        slope[:, cols] = cdf + pre * (jnp.exp(-0.5 * pre * pre) * (1.0 / math.sqrt(2.0 * math.pi)))
    pair = 2 * (width // HEADS)
    first_half = half_lanes(pair)
    for head in range(HEADS):
        cols = slice(head // 2 * pair, (head // 2 + 1) * pair)
        own = first_half if head % 2 == 0 else ~first_half
        for i, rows in causal_blocks(tokens, 256):
            here = slice(i, i + rows)
            keys = key_feat[here, cols]
            scores = mm(jnp.where(own, keys, jnp.zeros_like(keys)), query_feat[i:, cols], NT)
            weights_t[head * tokens + i : head * tokens + i + rows, i:] = (scores * mask_t[here, i:]).astype(bf16)


def slopes(query_feat, key_feat, mask_t, pre_act):
    tokens, width = query_feat.shape
    return pl.pallas_call(
        slopes_kernel,
        out_shape=[near((HEADS * tokens, tokens), bf16)]
        + [near((tokens, width), bf16)] * 2
        + [near(pre_act.shape, f32)],
        compiler_params=params(16),
        cost_estimate=NO_COST,
        name="slopes",
    )(*all_vmem((query_feat, key_feat, mask_t, pre_act)))


def middle_kernel(part0, part1, part2, part3, own_first, cotangent, vec, block_out, d_second, sums, *d_branch):
    branch = part0[...] + part1[...].astype(f32) + part2[...].astype(f32) + part3[...].astype(f32)
    unit, spread = norm_parts(own_first[...] + branch)
    gain = vec[2:3, :]
    block_out[...] = unit * gain + vec[3:4, :]
    grad = cotangent[...].astype(f32)
    inner = norm_back(grad, unit, spread, gain)
    d_second[...] = inner
    for copy in d_branch:
        copy[...] = inner.astype(bf16)
    sums[...] = jnp.zeros_like(sums)
    sums[2:3, :] = jnp.sum(grad * unit, axis=0, keepdims=True)
    sums[3:4, :] = jnp.sum(grad, axis=0, keepdims=True)


def middle(parts, own_first, cotangent, vec, held):
    local, width = own_first.shape
    return pl.pallas_call(
        holding(middle_kernel, 7, len(held)),
        out_shape=[near((local, width), f32), near((local, width), f32), near((8, width), f32)]
        + [near((local, width), bf16)] * 4,
        compiler_params=params(8),
        name="middle",
    )(in_vmem(parts[0]), *parts[1:], in_vmem(own_first), cotangent, vec, *all_vmem(held))


def feed_back_kernel(
    local, d0, d1, d2, d3, slope, up_low, down_low, d_branch, d_pre, part0, part1, part2, part3, total
):
    rank = lax.axis_index("mp")
    tokens, width = d_branch.shape
    ranks = tokens // local

    for step, block in zip(BACK_STEPS, (d0, d1, d2, d3)):
        d_branch[rank_rows(source(rank, step, ranks), local), :] = block[...]
    piece = 256
    for c in range(0, d_pre.shape[1], piece):
        cols = slice(c, c + piece)
        d_pre[:, cols] = (mm(d_branch[...], down_low[cols, :], NT) * slope[:, cols]).astype(bf16)
    total[...] = mm(d_pre[...], up_low[...], NT)
    for step, part in zip(FIRST_STEPS, (part0, part1, part2, part3)):
        part[...] = total[rank_rows(target(rank, step, ranks), local), :].astype(part.dtype)


def feed_back(blocks, slope, up_low, down_low, held):
    local, width = blocks[0].shape
    tokens, hidden = slope.shape
    return pl.pallas_call(
        holding(functools.partial(feed_back_kernel, local), 7, len(held)),
        out_shape=[near((tokens, width), bf16), near((tokens, hidden), bf16), near((local, width), f32)]
        + [near((local, width), bf16)] * 3,
        scratch_shapes=[pltpu.VMEM((tokens, width), f32)],
        compiler_params=params(16),
        cost_estimate=pl.CostEstimate(flops=1_200_000_000, bytes_accessed=9_000_000, transcendentals=0),
        name="feed_back",
    )(in_vmem(blocks[0]), *blocks[1:], *all_vmem((slope, up_low, down_low, *held)))


def feed_grads_kernel(first_low, d_pre, hidden_low, d_branch, keep_up, keep_down, send_up, send_down):
    for left, right, keep, send in (
        (first_low, d_pre, keep_up, send_up),
        (hidden_low, d_branch, keep_down, send_down),
    ):
        keep[...] = mm(left[:, half_rows(left.shape[1], True)], right[...], TN)
        send[...] = mm(left[:, half_rows(left.shape[1], False)], right[...], TN).astype(bf16)


def feed_grads(first_low, d_pre, hidden_low, d_branch):
    width, hidden = first_low.shape[1], d_pre.shape[1]
    return pl.pallas_call(
        feed_grads_kernel,
        out_shape=[near((width // 2, hidden), f32), near((hidden // 2, width), f32)]
        + [near((width // 2, hidden), bf16), near((hidden // 2, width), bf16)],
        compiler_params=params(16),
        cost_estimate=NO_COST,
        name="feed_grads",
    )(*all_vmem((first_low, d_pre, hidden_low, d_branch)))


def first_back_kernel(part0, part1, part2, part3, d_second, own_sum, sums_in, vec, d_resid, sums, *d_attn):
    grad = d_second[...] + part0[...] + part1[...].astype(f32) + part2[...].astype(f32) + part3[...].astype(f32)
    unit, spread = norm_parts(own_sum[...])
    inner = norm_back(grad, unit, spread, vec[0:1, :])
    d_resid[...] = inner
    for copy in d_attn:
        copy[...] = inner.astype(bf16)
    sums[...] = sums_in[...]
    sums[0:1, :] = jnp.sum(grad * unit, axis=0, keepdims=True)
    sums[1:2, :] = jnp.sum(grad, axis=0, keepdims=True)


def first_back(parts, d_second, own_sum, sums, vec, held):
    local, width = own_sum.shape
    return pl.pallas_call(
        holding(first_back_kernel, 8, len(held)),
        out_shape=[near((local, width), f32), near((8, width), f32)] + [near((local, width), bf16)] * 4,
        compiler_params=params(8),
        name="first_back",
    )(in_vmem(parts[0]), *parts[1:], *all_vmem((d_second, own_sum, sums)), vec, *all_vmem(held))


def own_columns_kernel(x_all, mixed_low, block_near, x_slice, mixed_slice, block_out, turned):
    block_out[...] = block_near[...]
    rows = x_slice.shape[0]
    mine = pl.ds(pl.multiple_of(lax.axis_index("mp") * rows, rows), rows)
    for source, target in ((x_all, x_slice), (mixed_low, mixed_slice)):
        turned[...] = jnp.transpose(source[...])
        target[...] = turned[mine, :]


def own_columns(x_all, mixed_low, block_near, own_width):
    tokens, width = x_all.shape
    return pl.pallas_call(
        own_columns_kernel,
        out_shape=[near((own_width, tokens), bf16)] * 2 + [sds(block_near.shape, f32)],
        scratch_shapes=[pltpu.VMEM((width, tokens), bf16)],
        compiler_params=params(8),
        cost_estimate=NO_COST,
        name="own_columns",
    )(*all_vmem((x_all, mixed_low, block_near)))


def mix_heads(
    start, d_num, d_den, query_feat, key_feat, value_low, query_slope, key_slope, weights_t, mask, mask_t, d_query, d_key,
    d_value,
):
    tokens, width = query_feat.shape
    pair = 2 * (width // HEADS)
    first_half = half_lanes(pair)
    spans = causal_blocks(tokens, 256)
    for c in range(start, start + width // 2, pair):
        cols = slice(c, c + pair)
        queries = query_feat[:, cols]
        keys = key_feat[:, cols]
        values = value_low[:, cols]
        nums = d_num[:, cols]
        left = jnp.concatenate([nums, d_den[:, cols]], axis=1)
        zero = jnp.zeros_like(keys)
        minus = jnp.full_like(values, -1)
        sides = (first_half, ~first_half)
        own_query = [jnp.where(own, queries, zero) for own in sides]
        own_key = [jnp.where(own, keys, zero) for own in sides]
        own_num = [jnp.where(own, nums, zero) for own in sides]
        right = [
            jnp.concatenate([jnp.where(own, values, zero), jnp.where(own, minus, zero)], axis=1) for own in sides
        ]
        base = 2 * (c // pair) * tokens
        out = slice(c - start, c - start + pair)
        for i, rows in spans:
            here = slice(i, i + rows)
            upto = i + rows
            allowed = mask[here, :upto]
            d_scores = mm(left[here], jnp.concatenate([block[:upto] for block in right], axis=0), NT)
            d_scores = (d_scores * jnp.concatenate([allowed, allowed], axis=1)).astype(bf16)
            grad = mm(d_scores, jnp.concatenate([block[:upto] for block in own_key], axis=0))
            d_query[here, out] = (grad * query_slope[here, cols].astype(f32)).astype(bf16)
            weights = jnp.concatenate(
                [weights_t[base + half * tokens + i : base + half * tokens + i + rows, i:] for half in range(2)], axis=1
            )
            grad = mm(weights, jnp.concatenate([block[i:] for block in own_num], axis=0))
            d_value[here, out] = grad.astype(bf16)
            allowed = mask_t[here, i:]
            d_scores_t = mm(jnp.concatenate([block[here] for block in right], axis=0), left[i:], NT)
            d_scores_t = [(d_scores_t[half * rows : (half + 1) * rows] * allowed).astype(bf16) for half in range(2)]
            grad = mm(
                jnp.concatenate(d_scores_t, axis=1), jnp.concatenate([block[i:] for block in own_query], axis=0)
            )
            d_key[here, out] = (grad * key_slope[here, cols].astype(f32)).astype(bf16)


def mix_first_kernel(
    local,
    a0,
    a1,
    a2,
    a3,
    attn_low,
    mixed_low,
    inverse,
    query_feat,
    key_feat,
    value_low,
    query_slope,
    key_slope,
    weights_t,
    mask,
    mask_t,
    d_attn,
    d_num,
    d_den,
    d_query,
    d_key,
    d_value,
):
    rank = lax.axis_index("mp")
    tokens, width = d_attn.shape
    ranks = tokens // local
    for step, block in zip(MIX_STEPS, (a0, a1, a2, a3)):
        d_attn[rank_rows(source(rank, step, ranks), local), :] = block[...]
    piece = 768
    for c in range(0, width, piece):
        cols = slice(c, c + piece)
        d_mixed = mm(d_attn[...], attn_low[3, cols, :], NT) * inverse[:, cols]
        d_num[:, cols] = d_mixed.astype(bf16)
        d_den[:, cols] = (d_mixed * mixed_low[:, cols].astype(f32)).astype(bf16)
    mix_heads(
        0, d_num, d_den, query_feat, key_feat, value_low, query_slope, key_slope, weights_t, mask, mask_t, d_query,
        d_key, d_value,
    )


def mix_first(blocks, attn_low, mixed_low, inverse, feats):
    local, width = blocks[0].shape
    tokens = mixed_low.shape[0]
    return pl.pallas_call(
        functools.partial(mix_first_kernel, local),
        out_shape=[near((tokens, width), bf16)] * 3 + [near((tokens, width // 2), bf16)] * 3,
        compiler_params=params(16),
        cost_estimate=pl.CostEstimate(flops=6_000_000_000, bytes_accessed=18_000_000, transcendentals=0),
        name="mix_first",
    )(in_vmem(blocks[0]), *blocks[1:], *all_vmem((attn_low, mixed_low, inverse, *feats)))


def mix_second_kernel(
    d_attn,
    d_num,
    d_den,
    first_query,
    first_key,
    first_value,
    attn_low,
    query_feat,
    key_feat,
    value_low,
    query_slope,
    key_slope,
    weights_t,
    mask,
    mask_t,
    x_slice,
    mixed_slice,
    sums,
    d_query,
    d_key,
    d_value,
    vec,
    keep,
    send,
    attn_grad,
):
    width = d_attn.shape[1]
    own_width = x_slice.shape[0]
    half = width // 2
    for source, target in ((first_query, d_query), (first_key, d_key), (first_value, d_value)):
        target[:, 0:half] = source[...]
    mix_heads(
        half, d_num, d_den, query_feat, key_feat, value_low, query_slope, key_slope, weights_t, mask, mask_t,
        d_query.at[:, half:width], d_key.at[:, half:width], d_value.at[:, half:width],
    )
    for k, grad in enumerate((d_query, d_key, d_value)):
        attn_grad[k * own_width : (k + 1) * own_width, :] = mm(x_slice[...], grad[...])
    attn_grad[3 * own_width : 4 * own_width, :] = mm(mixed_slice[...], d_attn[...])
    write_halves(attn_grad, keep, send)
    held, packed = two_parts(sums[0:4, :])
    send[2 * own_width :, :] = packed
    vec[0:4, :] = held
    vec[4:8, :] = jnp.zeros_like(held)


def mix_second(first, attn_low, feats, x_slice, mixed_slice, sums):
    tokens, width = first[0].shape
    own_width = x_slice.shape[0]
    return pl.pallas_call(
        mix_second_kernel,
        out_shape=[near((tokens, width), bf16)] * 3
        + [
            near((8, width), f32),
            near((2 * own_width, width), f32),
            near((2 * own_width + VEC_ROWS, width), bf16),
        ],
        scratch_shapes=[pltpu.VMEM((4 * own_width, width), f32)],
        compiler_params=params(16),
        cost_estimate=pl.CostEstimate(flops=6_000_000_000, bytes_accessed=18_000_000, transcendentals=0),
        name="mix_second",
    )(*all_vmem((*first, attn_low, *feats, x_slice, mixed_slice, sums)))


def tokens_back_kernel(
    d_query, d_key, d_value, attn_low, d_resid, attn_weight, up_weight, down_weight, tokens_grad, own_attn, own_up, own_down,
    sems,
):
    local, own_width = d_resid.shape[0], own_attn.shape[1]
    rank = lax.axis_index("mp")
    columns = pl.ds(pl.multiple_of(rank * own_width, own_width), own_width)
    copies = [
        pltpu.make_async_copy(attn_weight.at[:, columns, :], own_attn, sems.at[0]),
        pltpu.make_async_copy(up_weight, own_up, sems.at[1]),
        pltpu.make_async_copy(down_weight, own_down, sems.at[2]),
    ]
    for copy in copies:
        copy.start()
    mine = pl.ds(pl.multiple_of(rank * local, local), local)
    tokens_grad[...] = (
        d_resid[...]
        + mm(d_query[mine, :], attn_low[0], NT)
        + mm(d_key[mine, :], attn_low[1], NT)
        + mm(d_value[mine, :], attn_low[2], NT)
    )
    for copy in copies:
        copy.wait()


def tokens_back(d_query, d_key, d_value, attn_low, d_resid, attn_weight, up_weight, down_weight, own_width):
    return pl.pallas_call(
        tokens_back_kernel,
        in_specs=[pl.BlockSpec(memory_space=pltpu.VMEM)] * 5 + [pl.BlockSpec(memory_space=pl.ANY)] * 3,
        out_shape=[
            sds(d_resid.shape, f32),
            near((4, own_width, d_resid.shape[1]), f32),
            near(up_weight.shape, f32),
            near(down_weight.shape, f32),
        ],
        scratch_shapes=[pltpu.SemaphoreType.DMA((3,))],
        compiler_params=params(16),
        cost_estimate=NO_COST,
        name="tokens_back",
    )(
        *all_vmem((d_query, d_key, d_value, attn_low, d_resid)), in_hbm(attn_weight), in_hbm(up_weight),
        in_hbm(down_weight),
    )


def as_row(column):
    return jnp.transpose(jnp.broadcast_to(column, (column.shape[0], 128)))[0:1, :]


def as_column(row):
    return jnp.transpose(jnp.broadcast_to(row, (128, row.shape[1])))[:, 0:1]


SHARE_ROWS = 32


def lane_scalars(values, width):
    lane = lax.broadcasted_iota(jnp.int32, (1, width), 1)
    row = jnp.zeros((1, width), f32)
    for k, value in enumerate(values):
        row = jnp.where(lane == k, value, row)
    return row


def lane_scalar(row, k):
    lane = lax.broadcasted_iota(jnp.int32, row.shape, 1)
    return jnp.sum(jnp.where(lane == k, row, 0.0), axis=1, keepdims=True)


def attn_stats_kernel(even, odd, vec, stats, feed_shares, total, rows_new, shares, columns, rows16):
    own_width, width = total.shape[0] // 4, total.shape[1]
    mine = pl.ds(pl.multiple_of(lax.axis_index("mp") * own_width, own_width), own_width)
    read_halves(even, odd, total)
    scalars = []
    for k in range(4):
        grad = total[k * own_width : (k + 1) * own_width, :]
        square = grad * grad
        columns[...] = as_column(stats[k, 0:1, :])
        rows = decay * columns[mine, :] + (1.0 - decay) * jnp.mean(square + tiny_square, axis=1, keepdims=True)
        rows_new[k : k + 1, :] = as_row(rows)
        rows16[k : k + 1, :] = jnp.sum(square + tiny_square, axis=0, keepdims=True)
        rows16[4 + k : 5 + k, :] = jnp.sum(square * (1.0 / rows), axis=0, keepdims=True)
        scalars.append(jnp.sum(rows, axis=0, keepdims=True))
    rows16[8:12, :] = vec[0:4, :]
    rows16[12:16, :] = feed_shares[0:4, :]
    shares[0:16, :] = rows16[...].astype(bf16)
    row = lane_scalars(scalars, width) + feed_shares[4:5, :]
    high = row.astype(bf16).astype(f32)
    low = (row - high).astype(bf16).astype(f32)
    shares[16:, :] = jnp.concatenate([high, low, jnp.zeros((SHARE_ROWS - 18, width), f32)], axis=0).astype(bf16)


def attn_stats_call(even, odd, vec, stats, feed_shares, own_width):
    width = even.shape[1]
    return pl.pallas_call(
        attn_stats_kernel,
        out_shape=[near((4 * own_width, width), f32), near((4, own_width), f32), near((SHARE_ROWS, width), bf16)],
        scratch_shapes=[pltpu.VMEM((width, 1), f32), pltpu.VMEM((16, width), f32)],
        compiler_params=params(16),
        name="attn_stats",
    )(in_vmem(even), odd, in_vmem(vec), stats, in_vmem(feed_shares))


def attn_out_kernel(total, rows, grad_out, rows_out):
    own_width = grad_out.shape[1]
    for k in range(4):
        grad_out[k] = total[k * own_width : (k + 1) * own_width, :]
    rows_out[...] = rows[...]


def attn_out(total, rows):
    own_width, width = rows.shape[1], total.shape[1]
    return pl.pallas_call(
        attn_out_kernel,
        out_shape=[sds((4, own_width, width), f32), sds((4, own_width), f32)],
        compiler_params=params(8),
        cost_estimate=NO_COST,
        name="attn_out",
    )(*all_vmem((total, rows)))


def feed_stats_kernel(mine, other, wide_old, squares, up_grad_out, down_grad_out, wide_out, grads, wide_new, shares):
    width, hidden = up_grad_out.shape
    for part, rows in enumerate((width, hidden)):
        half = slice(part * width // 2, (part * width + rows) // 2)
        read_halves(mine.at[half], other.at[half], grads.at[part * width : part * width + rows])
    grad = grads[0:width, :]
    up_grad_out[...] = grad
    square = grad * grad
    columns = decay * wide_old[0:1, :] + (1.0 - decay) * jnp.mean(square + tiny_square, axis=0, keepdims=True)
    wide_new[0:1, :] = columns
    shares[0:1, :] = as_row(jnp.sum(square + tiny_square, axis=1, keepdims=True))
    shares[1:2, :] = as_row(jnp.sum(square * (1.0 / columns), axis=1, keepdims=True))
    grad = grads[width:, :]
    down_grad_out[...] = grad
    square = grad * grad
    rows = decay * as_column(wide_old[1:2, :]) + (1.0 - decay) * jnp.mean(
        square + tiny_square, axis=1, keepdims=True
    )
    wide_new[1:2, :] = as_row(rows)
    wide_out[...] = wide_new[...]
    shares[2:3, :] = jnp.sum(square + tiny_square, axis=0, keepdims=True)
    shares[3:4, :] = jnp.sum(square * (1.0 / rows), axis=0, keepdims=True)
    scalars = [jnp.sum(rows, axis=0, keepdims=True)]
    for k in range(2):
        scalars.append(jnp.sum(squares[4 + k : 5 + k, :], axis=1, keepdims=True))
    shares[4:5, :] = lane_scalars([0.0] * 4 + scalars, width)
    shares[5:8, :] = jnp.zeros((3, width), f32)


def feed_stats(even, odd, wide_old, squares):
    width, hidden = squares.shape[1], wide_old.shape[1]
    return pl.pallas_call(
        feed_stats_kernel,
        out_shape=[
            sds((width, hidden), f32),
            sds((hidden, width), f32),
            sds((2, hidden), f32),
            near((width + hidden, width), f32),
            near((2, hidden), f32),
            near((8, width), f32),
        ],
        compiler_params=params(16),
        cost_estimate=NO_COST,
        name="feed_stats",
    )(in_vmem(even), odd, wide_old, in_vmem(squares))


def update_kernel(
    hidden_all,
    attn_grad,
    attn_weight,
    attn_rows,
    stats,
    feed_grad,
    up_weight,
    down_weight,
    wide_new,
    narrow_old,
    squares,
    share,
    share1,
    share2,
    share3,
    vec,
    vec_moment,
    *refs,
):
    outs, made, sems = refs[0:11], refs[11:22], refs[22]
    attn_new, attn_new_low, up_new, up_new_low, down_new, down_new_low = made[0:6]
    attn_cols, narrow_new, vec_grad, vec_moment_new, vec_new = made[6:11]
    width = narrow_old.shape[1]
    own_width = attn_rows.shape[1]
    copies = []

    def leave(which, *place):
        source = made[which].at[place] if place else made[which]
        target = outs[which].at[place] if place else outs[which]
        copy = pltpu.make_async_copy(source, target, sems.at[len(copies)])
        copy.start()
        copies.append(copy)

    total = (share[...].astype(f32) + share1[...].astype(f32)) + (share2[...].astype(f32) + share3[...].astype(f32))
    scalars = total[16:17, :] + total[17:18, :]
    entries = float(width * hidden_all)
    rows = decay * narrow_old[0:1, :] + (1.0 - decay) * total[12:13, :] / hidden_all
    narrow_new[0:1, :] = rows
    cols = decay * narrow_old[1:2, :] + (1.0 - decay) * total[14:15, :] / hidden_all
    narrow_new[1:2, :] = cols
    mean_up = jnp.mean(rows, axis=1, keepdims=True)
    mean_down = lane_scalar(scalars, 4) / hidden_all

    def step_size(scaled, weight_square, count):
        clip = jnp.maximum(1.0, jnp.sqrt(scaled / count) / clip_limit)
        return learn_rate * jnp.sqrt(weight_square / count) / clip

    up_size = step_size(
        jnp.sum(total[13:14, :] / rows, axis=1, keepdims=True) * mean_up, lane_scalar(scalars, 5), entries
    )
    down_size = step_size(
        jnp.sum(total[15:16, :] / cols, axis=1, keepdims=True) * mean_down, lane_scalar(scalars, 6), entries
    )

    def block(which, here, grad, weight, row, col, mean, size):
        scale = row * col * (1.0 / mean)
        value = weight - size * (grad * lax.rsqrt(scale))
        made[which][here] = value
        made[which + 1][here] = value.astype(bf16)
        leave(which, *here)
        leave(which + 1, *here)

    pieces = 4
    row = as_column(rows)
    step = up_weight.shape[0] // pieces
    for n in range(pieces):
        here = slice(n * step, (n + 1) * step)
        block(2, (here, slice(None)), feed_grad[here, :], up_weight[here, :], row[here], wide_new[0:1, :], mean_up, up_size)
    row = as_column(wide_new[1:2, :])
    step = down_weight.shape[0] // pieces
    for n in range(pieces):
        here = slice(n * step, (n + 1) * step)
        below = slice(up_weight.shape[0] + n * step, up_weight.shape[0] + (n + 1) * step)
        block(4, (here, slice(None)), feed_grad[below, :], down_weight[here, :], row[here], cols, mean_down, down_size)
    leave(7)
    entries = float(width * width)
    for k in range(4):
        col = decay * stats[k, 1:2, :] + (1.0 - decay) * total[k : k + 1, :] / width
        attn_cols[k : k + 1, :] = col
        mean = lane_scalar(scalars, k) / width
        size = step_size(
            jnp.sum(total[4 + k : 5 + k, :] / col, axis=1, keepdims=True) * mean,
            jnp.sum(squares[k : k + 1, :], axis=1, keepdims=True),
            entries,
        )
        block(
            0, (k,), attn_grad[k * own_width : (k + 1) * own_width, :], attn_weight[k], as_column(attn_rows[k : k + 1, :]),
            col, mean, size,
        )
    leave(6)
    grads = total[8:12, :]
    vec_grad[...] = grads
    leave(8)
    moment = decay * vec_moment[...] + (1.0 - decay) * (grads * grads + tiny_square)
    vec_moment_new[...] = moment
    leave(9)
    scaled = grads * lax.rsqrt(moment)
    clip = jnp.maximum(1.0, jnp.sqrt(jnp.mean(scaled * scaled, axis=1, keepdims=True)) / clip_limit)
    held = vec[...]
    spread = jnp.sqrt(jnp.mean(held * held, axis=1, keepdims=True))
    vec_new[...] = held - learn_rate * spread * scaled / clip
    leave(10)
    for copy in copies:
        copy.wait()


def update(
    attn_grad, attn_weight, attn_rows, stats, feed_grad, up_weight, down_weight, wide_new, narrow_old, squares, shares,
    vec, vec_moment, hidden_all,
):
    _, own_width, width = attn_weight.shape
    hidden = up_weight.shape[1]
    outs = [((4, own_width, width), t) for t in (f32, bf16)]
    outs += [((width, hidden), t) for t in (f32, bf16)] + [((hidden, width), t) for t in (f32, bf16)]
    outs += [((4, width), f32), ((2, width), f32)] + [((4, width), f32)] * 3
    return pl.pallas_call(
        functools.partial(update_kernel, hidden_all),
        in_specs=[pl.BlockSpec(memory_space=pltpu.VMEM)] * 16,
        out_specs=[pl.BlockSpec(memory_space=pl.ANY)] * 11,
        out_shape=[pltpu.HBM(*out) for out in outs],
        scratch_shapes=[pltpu.VMEM(*out) for out in outs]
        + [pltpu.SemaphoreType.DMA((29,))],
        compiler_params=params(24),
        name="update",
    )(
        *all_vmem((attn_grad, attn_weight, attn_rows)), stats,
        *all_vmem((feed_grad, up_weight, down_weight, wide_new)), narrow_old, in_vmem(squares), in_vmem(shares[0]),
        *shares[1:], vec, vec_moment,
    )


def exchange(parts, steps):
    ranks = len(parts)
    moved = [
        lax.ppermute(part, "mp", [(i, target(i, step, ranks)) for i in range(ranks)])
        for part, step in zip(parts[1:], steps[1:])
    ]
    return [parts[0]] + moved


def on_device(
    tokens,
    cotangent,
    seq_starts,
    attn_weight,
    up_weight,
    down_weight,
    vec_params,
    attn_stats,
    ffn_narrow_stats,
    ffn_wide_stats,
    vec_moment,
):
    ranks = lax.axis_size("mp")
    local, width = tokens.shape
    own_width = width // ranks
    hidden_all = up_weight.shape[1] * ranks

    blocks = exchange([tokens] * ranks, TOKEN_STEPS)
    attn_low, up_low, down_low, mask, mask_t, squares = prepare(
        seq_starts, attn_weight, up_weight, down_weight, local * ranks
    )
    (
        x_all,
        query_feat,
        key_feat,
        value_low,
        mixed_low,
        inverse,
        own_sum,
        own_first,
        first_low,
        pre_act,
        hidden_low,
        *parts,
    ) = forward(blocks, attn_low, up_low, down_low, mask, vec_params)
    parts = exchange(parts, BRANCH_STEPS)
    weights_t, query_slope, key_slope, slope = slopes(query_feat, key_feat, mask_t, pre_act)
    own_first, slope = lax.optimization_barrier((own_first, slope))
    feats = (query_feat, key_feat, value_low, query_slope, key_slope, weights_t, mask, mask_t)
    mixing = (attn_low, mixed_low, inverse, *feats)
    feeding = (up_low, down_low, first_low, slope, hidden_low)
    block_near, d_second, sums, *d_branch = middle(
        parts, own_first, cotangent, vec_params, (*mixing, *feeding, own_sum, x_all)
    )
    turned_from, d_second = lax.optimization_barrier((x_all, d_second))
    x_slice, mixed_slice, block_out = own_columns(turned_from, mixed_low, block_near, own_width)
    slope, x_slice = lax.optimization_barrier((slope, x_slice))
    d_branch, d_pre, *parts = feed_back(
        exchange(d_branch, BACK_STEPS), slope, up_low, down_low, (*mixing, first_low, hidden_low, own_sum, d_second, sums, x_slice, mixed_slice)
    )
    staged = lax.axis_size("dp") == STAGED

    parts = exchange(parts, FIRST_STEPS)
    *feed_keep, up_send, down_send = feed_grads(first_low, d_pre, hidden_low, d_branch)
    if staged:
        up = fold_first(feed_keep[0], across(up_send, 1))
        down = fold_first(feed_keep[1], across(down_send, 1))
        parts[0], up, down = lax.optimization_barrier((parts[0], up, down))
        got_up, got_down = [[across(a, 2), across(b, 4)] for a, b in (up, down)]
    d_resid, sums, *d_attn = first_back(
        parts, d_second, own_sum, sums, vec_params, (*mixing, x_slice, mixed_slice)
    )
    blocks = exchange(d_attn, MIX_STEPS)
    if staged:
        d_resid, up, down = lax.optimization_barrier((d_resid, up, down))
        feed_a, feed_b = fold_feed((*up, *down), (*got_up, *got_down))
        blocks[0], feed_a, feed_b = lax.optimization_barrier((blocks[0], feed_a, feed_b))
        got_a, got_b = across(feed_a, 4), across(feed_b, 2)
    first = mix_first(blocks, attn_low, mixed_low, inverse, feats)
    *d_mix, vec_part, attn_keep, attn_send = mix_second(first, attn_low, feats, x_slice, mixed_slice, sums)
    if staged:
        feed_even = fold_feed_last(feed_a, got_a, feed_b, got_b)
        attn_send, feed_even = lax.optimization_barrier((attn_send, feed_even))
        received = across(attn_send, 1)
        feed_odd = across(feed_even, 1)
        vec_part, attn_a, attn_b = fold_first(attn_keep, received, vec_part)
        got_a, got_b = across(attn_a, 2), across(attn_b, 4)
    else:
        feed_even, feed_odd, attn_even, attn_odd, vec_part = lax.psum(
            (jnp.concatenate(feed_keep), jnp.concatenate([up_send, down_send]).astype(f32), attn_keep, attn_send[: 2 * own_width].astype(f32), vec_part), "dp"
        )
    up_grad, down_grad, wide_out, feed_near, wide_near, feed_shares = feed_stats(
        feed_even, feed_odd, ffn_wide_stats, squares
    )
    tokens_grad, own_attn, own_up, own_down = tokens_back(
        *d_mix, attn_low, d_resid, attn_weight, up_weight, down_weight, own_width
    )
    if staged:
        attn_a, feed_shares = lax.optimization_barrier((attn_a, feed_shares))
        vec_part, attn_a, attn_b = fold_second(attn_a, got_a, attn_b, got_b, vec_part)
        got_a, got_b = across(attn_a, 4), across(attn_b, 2)
        attn_a, tokens_grad = lax.optimization_barrier((attn_a, tokens_grad))
        vec_part, attn_even = fold_last(attn_a, got_a, attn_b, got_b, vec_part)
        attn_odd = across(attn_even, 1)
    attn_near, rows_near, shares = attn_stats_call(attn_even, attn_odd, vec_part, attn_stats, feed_shares, own_width)
    shares = exchange([shares] * ranks, SHARE_STEPS)
    attn_grad, attn_rows = attn_out(attn_near, rows_near)
    attn_near, attn_grad = lax.optimization_barrier((attn_near, attn_grad))
    (
        attn_new,
        attn_new_low,
        up_new,
        up_new_low,
        down_new,
        down_new_low,
        attn_cols,
        narrow_new,
        vec_grad,
        vec_moment_new,
        vec_new,
    ) = update(
        attn_near, own_attn, rows_near, attn_stats, feed_near, own_up, own_down, wide_near, ffn_narrow_stats,
        squares, shares, vec_params, vec_moment, hidden_all,
    )
    return (
        block_out,
        tokens_grad,
        attn_grad,
        attn_rows,
        attn_cols,
        attn_new,
        attn_new_low,
        up_grad,
        down_grad,
        narrow_new,
        wide_out,
        up_new,
        down_new,
        up_new_low,
        down_new_low,
        vec_grad,
        vec_moment_new,
        vec_new,
    )


def solution(mesh):
    in_specs = (
        P(("dp", "mp"), None),
        P(("dp", "mp"), None),
        P("dp", None),
        P(),
        P(None, "mp"),
        P("mp", None),
        P(),
        P(),
        P(),
        P(None, "mp"),
        P(),
    )
    out_specs = (
        P(("dp", "mp"), None),
        P(("dp", "mp"), None),
        P(None, "mp", None),
        P(None, "mp"),
        P(),
        P(None, "mp", None),
        P(None, "mp", None),
        P(None, "mp"),
        P("mp", None),
        P(),
        P(None, "mp"),
        P(None, "mp"),
        P("mp", None),
        P(None, "mp"),
        P("mp", None),
        P(),
        P(),
        P(),
    )
    return jax.shard_map(
        on_device, mesh=mesh, in_specs=in_specs, out_specs=out_specs, check_vma=False
    )
```

profile of v0, /device:TPU:0, one launch (start us, length us, event | category | flops | bytes accessed | tf_op | source)
XLA Modules:
  0.0 157.6 jit_solution(348994165567976629)
XLA Ops:
  0.7 3.1 %collective-permute-start.1 = (bf16[128,768]{1,0:T(8,128)(2,1)}, bf16[128,768]{1,0:T(8,128)(2,1)S(1)}, u32[]{:S(2)}, u32[]{:S(2)}) collective-permute-start(bf16[128,768]{1,0:T(8,128)(2,1)} %x0.1), channel_id=1, source_target_pairs={{0,1},{1,0},{2,3},{3,2},{4,5},{5,4},{6,7},{7,6},{8,9},{9,8},{10,11... | collective-permute-start | bytes 589832 | tf_op jit(solution)/shard_map/ppermute | solution.py:1067
  3.8 2.6 %collective-permute-start = (bf16[128,768]{1,0:T(8,128)(2,1)}, bf16[128,768]{1,0:T(8,128)(2,1)S(1)}, u32[]{:S(2)}, u32[]{:S(2)}) collective-permute-start(bf16[128,768]{1,0:T(8,128)(2,1)} %x0.1), channel_id=1, source_target_pairs={{0,2},{1,3},{2,0},{3,1},{4,6},{5,7},{6,4},{7,5},{8,10},{9,11},{10,... | collective-permute-start | bytes 589832 | tf_op jit(solution)/shard_map/ppermute | solution.py:1067
  6.3 0.7 copy-done.6
  7.0 8.8 %prepare.1 = (bf16[4,768,768]{2,1,0:T(8,128)(2,1)S(1)}, bf16[768,768]{1,0:T(8,128)(2,1)S(1)}, bf16[768,768]{1,0:T(8,128)(2,1)S(1)}, f32[512,512]{1,0:T(8,128)S(1...) custom-call(s32[1,8]{1,0:T(1,128)S(1)} %copy-done.6, f32[4,768,768]{2,1,0:T(8,128)} %attn_weight.1, ...), custom_call_target="tpu_custom_call" | custom-call | flops 10000000 | bytes 22000000 | tf_op jit(solution)/shard_map/prepare/pallas_call | solution.py:275
  15.9 5.3 %collective-permute-done.x1 = bf16[128,768]{1,0:T(8,128)(2,1)S(1)} collective-permute-done((bf16[128,768]{1,0:T(8,128)(2,1)}, bf16[128,768]{1,0:T(8,128)(2,1)S(1)}, u32[]{:S(2)}, u32[]{:S(2)}) %collective-permute-start) | collective-permute-done | bytes 196640 | tf_op jit(solution)/shard_map/ppermute | solution.py:1067
  21.1 8.1 %forward.1 = (bf16[512,768]{1,0:T(8,128)(2,1)S(1)}, bf16[512,768]{1,0:T(8,128)(2,1)S(1)}, bf16[512,768]{1,0:T(8,128)(2,1)S(1)}, bf16[512,768]{1,0:T(8,128)(2,1)S...) custom-call(bf16[128,768]{1,0:T(8,128)(2,1)S(1)} %copy-done.7, ...), custom_call_target="tpu_custom_call" | custom-call | flops 8000000000 | bytes 20000000 | tf_op jit(solution)/shard_map/forward/pallas_call | solution.py:424
  29.3 3.4 %collective-permute-start.3 = (bf16[128,768]{1,0:T(8,128)(2,1)S(1)}, bf16[128,768]{1,0:T(8,128)(2,1)S(1)}, u32[]{:S(2)}, u32[]{:S(2)}) collective-permute-start(bf16[128,768]{1,0:T(8,128)(2,1)S(1)} %get-tuple-element.154), channel_id=1, source_target_pairs={{0,1},{1,2},{2,3},{3,0},{4,5},{5,6},{6,7},{7,4},{8,9},{9,10},{10,1... | collective-permute-start | bytes 589832 | tf_op jit(solution)/shard_map/ppermute | solution.py:1067
  32.7 1.1 collective-permute-start.4
  33.8 2.8 %collective-permute-start.5 = (bf16[128,768]{1,0:T(8,128)(2,1)S(1)}, bf16[128,768]{1,0:T(8,128)(2,1)S(1)}, u32[]{:S(2)}, u32[]{:S(2)}) collective-permute-start(bf16[128,768]{1,0:T(8,128)(2,1)S(1)} %get-tuple-element.156), channel_id=1, source_target_pairs={{0,3},{1,0},{2,1},{3,2},{4,7},{5,4},{6,5},{7,6},{8,11},{9,8},{10,9... | collective-permute-start | bytes 589832 | tf_op jit(solution)/shard_map/ppermute | solution.py:1067
  36.6 4.3 %slopes.1 = (bf16[6144,512]{1,0:T(8,128)(2,1)S(1)}, bf16[512,768]{1,0:T(8,128)(2,1)S(1)}, bf16[512,768]{1,0:T(8,128)(2,1)S(1)}, f32[512,768]{1,0:T(8,128)S(1)}) custom-call(bf16[512,768]{1,0:T(8,128)(2,1)S(1)} %get-tuple-element.158.query_feat.refs_10_.refs_11_, bf16[512,768]{1,0:T(8,128)(2,1)S(1)} %get-tuple-element.159.key_feat.refs_11_.refs_12_, ...), custom_call_target="tpu_custom_call" | custom-call | tf_op jit(solution)/shard_map/slopes/pallas_call | solution.py:466
  40.9 4.4 %collective-permute-done.4.refs_2_ = bf16[128,768]{1,0:T(8,128)(2,1)S(1)} collective-permute-done((bf16[128,768]{1,0:T(8,128)(2,1)S(1)}, bf16[128,768]{1,0:T(8,128)(2,1)S(1)}, u32[]{:S(2)}, u32[]{:S(2)}) %collective-permute-start.4) | collective-permute-done | bytes 196640 | tf_op jit(solution)/shard_map/ppermute | solution.py:1067
  45.3 0.4 middle.1
  45.8 4.5 %collective-permute-start.6 = (bf16[128,768]{1,0:T(8,128)(2,1)S(1)}, bf16[128,768]{1,0:T(8,128)(2,1)S(1)}, u32[]{:S(2)}, u32[]{:S(2)}) collective-permute-start(bf16[128,768]{1,0:T(8,128)(2,1)S(1)} %get-tuple-element.179), channel_id=1, source_target_pairs={{0,2},{1,3},{2,0},{3,1},{4,6},{5,7},{6,4},{7,5},{8,10},{9,11},{10,... | collective-permute-start | bytes 589832 | tf_op jit(solution)/shard_map/ppermute | solution.py:1067
  50.2 3.5 %collective-permute-start.7 = (bf16[128,768]{1,0:T(8,128)(2,1)S(1)}, bf16[128,768]{1,0:T(8,128)(2,1)S(1)}, u32[]{:S(2)}, u32[]{:S(2)}) collective-permute-start(bf16[128,768]{1,0:T(8,128)(2,1)S(1)} %get-tuple-element.180), channel_id=1, source_target_pairs={{0,1},{1,2},{2,3},{3,0},{4,5},{5,6},{6,7},{7,4},{8,9},{9,10},{10,1... | collective-permute-start | bytes 589832 | tf_op jit(solution)/shard_map/ppermute | solution.py:1067
  53.8 0.3 collective-permute-start.8
  54.1 1.2 own_columns.1
  55.2 8.6 %collective-permute-done.6.refs_1_ = bf16[128,768]{1,0:T(8,128)(2,1)S(1)} collective-permute-done((bf16[128,768]{1,0:T(8,128)(2,1)S(1)}, bf16[128,768]{1,0:T(8,128)(2,1)S(1)}, u32[]{:S(2)}, u32[]{:S(2)}) %collective-permute-start.6) | collective-permute-done | bytes 196640 | tf_op jit(solution)/shard_map/ppermute | solution.py:1067
  63.8 0.2 collective-permute-done.8.refs_3_
  64.1 1.7 %feed_back.1 = (bf16[512,768]{1,0:T(8,128)(2,1)S(1)}, bf16[512,768]{1,0:T(8,128)(2,1)S(1)}, f32[128,768]{1,0:T(8,128)S(1)}, bf16[128,768]{1,0:T(8,128)(2,1)S(1)}...) custom-call(bf16[128,768]{1,0:T(8,128)(2,1)S(1)} %get-tuple-element.178.refs_0_, ...), custom_call_target="tpu_custom_call" | custom-call | flops 1200000000 | bytes 9000000 | tf_op jit(solution)/shard_map/feed_back/pallas_call | solution.py:524
  65.7 1.4 feed_grads.1
  67.2 0.5 collective-permute-start.10
  67.7 3.8 %collective-permute-start.11 = (bf16[128,768]{1,0:T(8,128)(2,1)S(1)}, bf16[128,768]{1,0:T(8,128)(2,1)S(1)}, u32[]{:S(2)}, u32[]{:S(2)}) collective-permute-start(bf16[128,768]{1,0:T(8,128)(2,1)S(1)} %get-tuple-element.200), channel_id=1, source_target_pairs={{0,1},{1,2},{2,3},{3,0},{4,5},{5,6},{6,7},{7,4},{8,9},{9,10},{10,1... | collective-permute-start | bytes 589832 | tf_op jit(solution)/shard_map/ppermute | solution.py:1067
  71.5 1.9 %collective-permute-start.12 = (bf16[128,768]{1,0:T(8,128)(2,1)S(1)}, bf16[128,768]{1,0:T(8,128)(2,1)S(1)}, u32[]{:S(2)}, u32[]{:S(2)}) collective-permute-start(bf16[128,768]{1,0:T(8,128)(2,1)S(1)} %get-tuple-element.201), channel_id=1, source_target_pairs={{0,2},{1,3},{2,0},{3,1},{4,6},{5,7},{6,4},{7,5},{8,10},{9,11},{10,... | collective-permute-start | bytes 589832 | tf_op jit(solution)/shard_map/ppermute | solution.py:1067
  73.6 1.5 collective-permute-start.14
  75.2 1.5 collective-permute-start.15
  76.7 2.9 %collective-permute-start.13 = (bf16[128,768]{1,0:T(8,128)(2,1)S(1)}, bf16[128,768]{1,0:T(8,128)(2,1)S(1)}, u32[]{:S(2)}, u32[]{:S(2)}) collective-permute-start(bf16[128,768]{1,0:T(8,128)(2,1)S(1)} %get-tuple-element.202), channel_id=1, source_target_pairs={{0,3},{1,0},{2,1},{3,2},{4,7},{5,4},{6,5},{7,6},{8,11},{9,8},{10,9... | collective-permute-start | bytes 589832 | tf_op jit(solution)/shard_map/ppermute | solution.py:1067
  79.6 0.5 collective-permute-start.16
  80.2 4.9 %collective-permute-done.12.refs_2_ = bf16[128,768]{1,0:T(8,128)(2,1)S(1)} collective-permute-done((bf16[128,768]{1,0:T(8,128)(2,1)S(1)}, bf16[128,768]{1,0:T(8,128)(2,1)S(1)}, u32[]{:S(2)}, u32[]{:S(2)}) %collective-permute-start.12) | collective-permute-done | bytes 196640 | tf_op jit(solution)/shard_map/ppermute | solution.py:1067
  85.0 1.5 collective-permute-start.17
  86.6 0.2 collective-permute-done.13.refs_3_
  86.7 0.4 first_back.1
  87.2 5.9 %collective-permute-start.18 = (bf16[128,768]{1,0:T(8,128)(2,1)S(1)}, bf16[128,768]{1,0:T(8,128)(2,1)S(1)}, u32[]{:S(2)}, u32[]{:S(2)}) collective-permute-start(bf16[128,768]{1,0:T(8,128)(2,1)S(1)} %get-tuple-element.216), channel_id=1, source_target_pairs={{0,2},{1,3},{2,0},{3,1},{4,6},{5,7},{6,4},{7,5},{8,10},{9,11},{10,... | collective-permute-start | bytes 589832 | tf_op jit(solution)/shard_map/ppermute | solution.py:1067
  93.1 3.3 %collective-permute-start.19 = (bf16[128,768]{1,0:T(8,128)(2,1)S(1)}, bf16[128,768]{1,0:T(8,128)(2,1)S(1)}, u32[]{:S(2)}, u32[]{:S(2)}) collective-permute-start(bf16[128,768]{1,0:T(8,128)(2,1)S(1)} %get-tuple-element.217), channel_id=1, source_target_pairs={{0,1},{1,2},{2,3},{3,0},{4,5},{5,6},{6,7},{7,4},{8,9},{9,10},{10,1... | collective-permute-start | bytes 589832 | tf_op jit(solution)/shard_map/ppermute | solution.py:1067
  96.4 0.5 collective-permute-start.20
  97.0 0.3 fold_feed.1
  97.2 0.6 collective-permute-start.21
  97.8 2.7 %collective-permute-start.22 = (bf16[384,768]{1,0:T(8,128)(2,1)S(1)}, bf16[384,768]{1,0:T(8,128)(2,1)S(1)}, u32[]{:S(2)}, u32[]{:S(2)}) collective-permute-start(bf16[384,768]{1,0:T(8,128)(2,1)S(1)} %get-tuple-element.229.own_b), channel_id=1, source_target_pairs={{0,8},{4,12},{8,0},{12,4},{16,24},{20,28},{24,16},{28,20},{1,9},{5... | collective-permute-start | bytes 1769480 | tf_op jit(solution)/shard_map/ppermute | solution.py:224
  100.5 5.7 %collective-permute-done.18.a1 = bf16[128,768]{1,0:T(8,128)(2,1)S(1)} collective-permute-done((bf16[128,768]{1,0:T(8,128)(2,1)S(1)}, bf16[128,768]{1,0:T(8,128)(2,1)S(1)}, u32[]{:S(2)}, u32[]{:S(2)}) %collective-permute-start.18) | collective-permute-done | bytes 196640 | tf_op jit(solution)/shard_map/ppermute | solution.py:1067
  106.1 0.7 collective-permute-done.20.a3
  106.8 4.3 %mix_first.1 = (bf16[512,768]{1,0:T(8,128)(2,1)S(1)}, bf16[512,768]{1,0:T(8,128)(2,1)S(1)}, bf16[512,768]{1,0:T(8,128)(2,1)S(1)}, bf16[512,384]{1,0:T(8,128)(2,1...) custom-call(bf16[128,768]{1,0:T(8,128)(2,1)S(1)} %get-tuple-element.215.a0, ...), custom_call_target="tpu_custom_call" | custom-call | flops 6000000000 | bytes 18000000 | tf_op jit(solution)/shard_map/mix_first/pallas_call | solution.py:691
  111.2 4.7 %mix_second.1 = (bf16[512,768]{1,0:T(8,128)(2,1)S(1)}, bf16[512,768]{1,0:T(8,128)(2,1)S(1)}, bf16[512,768]{1,0:T(8,128)(2,1)S(1)}, f32[8,768]{1,0:T(8,128)S(1)},...) custom-call(bf16[512,768]{1,0:T(8,128)(2,1)S(1)} %get-tuple-element.219.d_attn, ...), custom_call_target="tpu_custom_call" | custom-call | flops 6000000000 | bytes 18000000 | tf_op jit(solution)/shard_map/mix_second/pallas_call | solution.py:749
  115.9 0.3 fold_feed_last.1.mine
  116.2 0.5 collective-permute-start.23
  116.7 3.2 %collective-permute-done.23.received = bf16[400,768]{1,0:T(8,128)(2,1)S(1)} collective-permute-done((bf16[400,768]{1,0:T(8,128)(2,1)S(1)}, bf16[400,768]{1,0:T(8,128)(2,1)S(1)}, u32[]{:S(2)}, u32[]{:S(2)}) %collective-permute-start.23) | collective-permute-done | bytes 614432 | tf_op jit(solution)/shard_map/ppermute | solution.py:224
  120.1 1.1 collective-permute-start.25
  121.2 0.5 collective-permute-start.26
  121.7 3.7 %feed_stats.1 = (f32[768,768]{1,0:T(8,128)}, f32[768,768]{1,0:T(8,128)}, f32[2,768]{1,0:T(2,128)}, f32[1536,768]{1,0:T(8,128)S(1)}, f32[2,768]{1,0:T(2,128)S(1)}, /*index=5*/f32[8,768]{1,0:T(8,128)S(1)}) custom-call(bf16[768,768]{1,0:T(8,128)(2,1)S(1)} %fold_feed_last.1.mine, bf16[768,768]{1,0:T(8,128)(2,1)S(1)} %collective-permute-done.24.other, ...), custom_call_target="tpu_custom_call" | custom-call | tf_op jit(solution)/shard_map/feed_stats/pallas_call | solution.py:916
  125.3 4.6 %collective-permute-done.26.got_b = bf16[192,768]{1,0:T(8,128)(2,1)S(1)} collective-permute-done((bf16[192,768]{1,0:T(8,128)(2,1)S(1)}, bf16[192,768]{1,0:T(8,128)(2,1)S(1)}, u32[]{:S(2)}, u32[]{:S(2)}) %collective-permute-start.26) | collective-permute-done | bytes 294944 | tf_op jit(solution)/shard_map/ppermute | solution.py:224
  129.9 0.1 fold_second.1
  130.1 0.8 collective-permute-start.27
  130.9 1.0 collective-permute-start.28
  131.9 4.6 %tokens_back.1 = (f32[128,768]{1,0:T(8,128)}, f32[4,192,768]{2,1,0:T(8,128)S(1)}, f32[768,768]{1,0:T(8,128)S(1)}, f32[768,768]{1,0:T(8,128)S(1)}) custom-call(bf16[512,768]{1,0:T(8,128)(2,1)S(1)} %get-tuple-element.240.d_query, bf16[512,768]{1,0:T(8,128)(2,1)S(1)} %get-tuple-element.241.d_key, bf16[512,768]{1,0:T(8,128)(2,1)S(1)} %get-tuple-element.242.d_value, ...), custom_call_target="tpu_custom_call" | custom-call | tf_op jit(solution)/shard_map/tokens_back/pallas_call | solution.py:790
  136.5 2.2 %collective-permute-done.28.got_b = bf16[192,768]{1,0:T(8,128)(2,1)S(1)} collective-permute-done((bf16[192,768]{1,0:T(8,128)(2,1)S(1)}, bf16[192,768]{1,0:T(8,128)(2,1)S(1)}, u32[]{:S(2)}, u32[]{:S(2)}) %collective-permute-start.28) | collective-permute-done | bytes 294944 | tf_op jit(solution)/shard_map/ppermute | solution.py:224
  138.6 0.3 collective-permute-done.27.got_a
  139.0 0.1 fold_last.1
  139.2 2.0 %collective-permute-done.29.odd = bf16[384,768]{1,0:T(8,128)(2,1)S(1)} collective-permute-done((bf16[384,768]{1,0:T(8,128)(2,1)S(1)}, bf16[384,768]{1,0:T(8,128)(2,1)S(1)}, u32[]{:S(2)}, u32[]{:S(2)}) %collective-permute-start.29) | collective-permute-done | bytes 589856 | tf_op jit(solution)/shard_map/ppermute | solution.py:224
  141.2 1.7 %attn_stats.1 = (f32[768,768]{1,0:T(8,128)S(1)}, f32[4,192]{1,0:T(4,128)S(1)}, bf16[32,768]{1,0:T(8,128)(2,1)S(1)}) custom-call(bf16[384,768]{1,0:T(8,128)(2,1)S(1)} %get-tuple-element.249.even, bf16[384,768]{1,0:T(8,128)(2,1)S(1)} %collective-permute-done.29.odd, f32[8,768]{1,0:T(8,128)S(1)} %get-tuple-element.250.vec, f32[4,2,768]{2,1,0:T(2,128)S(1)} %copy-done.2, ...), custom_call_target="tpu_custom_call" | custom-call | tf_op jit(solution)/shard_map/attn_stats/pallas_call | solution.py:858
  142.8 3.8 %collective-permute-start.32 = (bf16[32,768]{1,0:T(8,128)(2,1)S(1)}, bf16[32,768]{1,0:T(8,128)(2,1)S(1)}, u32[]{:S(2)}, u32[]{:S(2)}) collective-permute-start(bf16[32,768]{1,0:T(8,128)(2,1)S(1)} %get-tuple-element.263.share), channel_id=1, source_target_pairs={{0,3},{1,2},{2,1},{3,0},{4,7},{5,6},{6,5},{7,4},{8,11},{9,10},{10,... | collective-permute-start | bytes 147464 | tf_op jit(solution)/shard_map/ppermute | solution.py:1067
  146.6 1.7 %collective-permute-start.31 = (bf16[32,768]{1,0:T(8,128)(2,1)S(1)}, bf16[32,768]{1,0:T(8,128)(2,1)S(1)}, u32[]{:S(2)}, u32[]{:S(2)}) collective-permute-start(bf16[32,768]{1,0:T(8,128)(2,1)S(1)} %get-tuple-element.263.share), channel_id=1, source_target_pairs={{0,2},{1,3},{2,0},{3,1},{4,6},{5,7},{6,4},{7,5},{8,10},{9,11},{10,... | collective-permute-start | bytes 147464 | tf_op jit(solution)/shard_map/ppermute | solution.py:1067
  148.4 0.5 collective-permute-start.30
  148.8 1.6 attn_out.1
  150.4 1.2 collective-permute-done.31.share2
  151.7 0.8 collective-permute-done.30.share1
  152.5 5.0 %update.1 = (f32[4,192,768]{2,1,0:T(8,128)}, bf16[4,192,768]{2,1,0:T(8,128)(2,1)}, f32[768,768]{1,0:T(8,128)}, bf16[768,768]{1,0:T(8,128)(2,1)}, f32[768,768]{1,...) custom-call(f32[768,768]{1,0:T(8,128)S(1)} %get-tuple-element.257.to, ...), custom_call_target="tpu_custom_call" | custom-call | tf_op jit(solution)/shard_map/update/pallas_call | solution.py:1048
  (40 shorter events, 0.6 us)
Async XLA Ops:
  0.7 20.5 %copy-start.1 = (f32[4,768]{1,0:T(4,128)S(1)}, f32[4,768]{1,0:T(4,128)}, u32[]{:S(2)}) copy-start(f32[4,768]{1,0:T(4,128)} %vec.3) | copy-start | bytes 36868
  0.7 15.2 %collective-permute-start.1 = (bf16[128,768]{1,0:T(8,128)(2,1)}, bf16[128,768]{1,0:T(8,128)(2,1)S(1)}, u32[]{:S(2)}, u32[]{:S(2)}) collective-permute-start(bf16[128,768]{1,0:T(8,128)(2,1)} %x0.1), channel_id=1, source_target_pairs={{0,1},{1,0},{2,3},{3,2},{4,5},{5,4},{6,7},{7,6},{8,9},{9,8},{10,11... | collective-permute-start | bytes 589832 | tf_op jit(solution)/shard_map/ppermute | solution.py:1067
  3.8 17.4 %collective-permute-start = (bf16[128,768]{1,0:T(8,128)(2,1)}, bf16[128,768]{1,0:T(8,128)(2,1)S(1)}, u32[]{:S(2)}, u32[]{:S(2)}) collective-permute-start(bf16[128,768]{1,0:T(8,128)(2,1)} %x0.1), channel_id=1, source_target_pairs={{0,2},{1,3},{2,0},{3,1},{4,6},{5,7},{6,4},{7,5},{8,10},{9,11},{10,... | collective-permute-start | bytes 589832 | tf_op jit(solution)/shard_map/ppermute | solution.py:1067
  6.3 14.8 %collective-permute-start.2 = (bf16[128,768]{1,0:T(8,128)(2,1)}, bf16[128,768]{1,0:T(8,128)(2,1)S(1)}, u32[]{:S(2)}, u32[]{:S(2)}) collective-permute-start(bf16[128,768]{1,0:T(8,128)(2,1)} %x0.1), channel_id=1, source_target_pairs={{0,3},{1,2},{2,1},{3,0},{4,7},{5,6},{6,5},{7,4},{8,11},{9,10},{10,... | collective-permute-start | bytes 589832 | tf_op jit(solution)/shard_map/ppermute | solution.py:1067
  6.3 0.7 copy-start.6
  7.0 14.1 %copy-start.7 = (bf16[128,768]{1,0:T(8,128)(2,1)S(1)}, bf16[128,768]{1,0:T(8,128)(2,1)}, u32[]{:S(2)}) copy-start(bf16[128,768]{1,0:T(8,128)(2,1)} %x0.1) | copy-start | bytes 589828
  29.3 16.1 %copy-start = (bf16[128,768]{1,0:T(8,128)(2,1)S(1)}, bf16[128,768]{1,0:T(8,128)(2,1)}, u32[]{:S(2)}) copy-start(bf16[128,768]{1,0:T(8,128)(2,1)} %refs_5_.1) | copy-start | bytes 589828
  29.3 11.6 %collective-permute-start.3 = (bf16[128,768]{1,0:T(8,128)(2,1)S(1)}, bf16[128,768]{1,0:T(8,128)(2,1)S(1)}, u32[]{:S(2)}, u32[]{:S(2)}) collective-permute-start(bf16[128,768]{1,0:T(8,128)(2,1)S(1)} %get-tuple-element.154), channel_id=1, source_target_pairs={{0,1},{1,2},{2,3},{3,0},{4,5},{5,6},{6,7},{7,4},{8,9},{9,10},{10,1... | collective-permute-start | bytes 589832 | tf_op jit(solution)/shard_map/ppermute | solution.py:1067
  32.7 12.6 %collective-permute-start.4 = (bf16[128,768]{1,0:T(8,128)(2,1)S(1)}, bf16[128,768]{1,0:T(8,128)(2,1)S(1)}, u32[]{:S(2)}, u32[]{:S(2)}) collective-permute-start(bf16[128,768]{1,0:T(8,128)(2,1)S(1)} %get-tuple-element.155), channel_id=1, source_target_pairs={{0,2},{1,3},{2,0},{3,1},{4,6},{5,7},{6,4},{7,5},{8,10},{9,11},{10,... | collective-permute-start | bytes 589832 | tf_op jit(solution)/shard_map/ppermute | solution.py:1067
  33.8 11.6 %collective-permute-start.5 = (bf16[128,768]{1,0:T(8,128)(2,1)S(1)}, bf16[128,768]{1,0:T(8,128)(2,1)S(1)}, u32[]{:S(2)}, u32[]{:S(2)}) collective-permute-start(bf16[128,768]{1,0:T(8,128)(2,1)S(1)} %get-tuple-element.156), channel_id=1, source_target_pairs={{0,3},{1,0},{2,1},{3,2},{4,7},{5,4},{6,5},{7,6},{8,11},{9,8},{10,9... | collective-permute-start | bytes 589832 | tf_op jit(solution)/shard_map/ppermute | solution.py:1067
  45.8 18.1 %collective-permute-start.6 = (bf16[128,768]{1,0:T(8,128)(2,1)S(1)}, bf16[128,768]{1,0:T(8,128)(2,1)S(1)}, u32[]{:S(2)}, u32[]{:S(2)}) collective-permute-start(bf16[128,768]{1,0:T(8,128)(2,1)S(1)} %get-tuple-element.179), channel_id=1, source_target_pairs={{0,2},{1,3},{2,0},{3,1},{4,6},{5,7},{6,4},{7,5},{8,10},{9,11},{10,... | collective-permute-start | bytes 589832 | tf_op jit(solution)/shard_map/ppermute | solution.py:1067
  50.2 13.6 %collective-permute-start.7 = (bf16[128,768]{1,0:T(8,128)(2,1)S(1)}, bf16[128,768]{1,0:T(8,128)(2,1)S(1)}, u32[]{:S(2)}, u32[]{:S(2)}) collective-permute-start(bf16[128,768]{1,0:T(8,128)(2,1)S(1)} %get-tuple-element.180), channel_id=1, source_target_pairs={{0,1},{1,2},{2,3},{3,0},{4,5},{5,6},{6,7},{7,4},{8,9},{9,10},{10,1... | collective-permute-start | bytes 589832 | tf_op jit(solution)/shard_map/ppermute | solution.py:1067
  53.8 10.3 %collective-permute-start.8 = (bf16[128,768]{1,0:T(8,128)(2,1)S(1)}, bf16[128,768]{1,0:T(8,128)(2,1)S(1)}, u32[]{:S(2)}, u32[]{:S(2)}) collective-permute-start(bf16[128,768]{1,0:T(8,128)(2,1)S(1)} %get-tuple-element.181), channel_id=1, source_target_pairs={{0,3},{1,0},{2,1},{3,2},{4,7},{5,4},{6,5},{7,6},{8,11},{9,8},{10,9... | collective-permute-start | bytes 589832 | tf_op jit(solution)/shard_map/ppermute | solution.py:1067
  67.2 6.3 %collective-permute-start.9 = (bf16[384,768]{1,0:T(8,128)(2,1)S(1)}, bf16[384,768]{1,0:T(8,128)(2,1)S(1)}, u32[]{:S(2)}, u32[]{:S(2)}) collective-permute-start(bf16[384,768]{1,0:T(8,128)(2,1)S(1)} %get-tuple-element.192), channel_id=1, source_target_pairs={{0,4},{4,0},{8,12},{12,8},{16,20},{20,16},{24,28},{28,24},{1,5},{5... | collective-permute-start | bytes 1769480 | tf_op jit(solution)/shard_map/ppermute | solution.py:224
  67.2 6.3 %collective-permute-start.10 = (bf16[384,768]{1,0:T(8,128)(2,1)S(1)}, bf16[384,768]{1,0:T(8,128)(2,1)S(1)}, u32[]{:S(2)}, u32[]{:S(2)}) collective-permute-start(bf16[384,768]{1,0:T(8,128)(2,1)S(1)} %get-tuple-element.196), channel_id=1, source_target_pairs={{0,4},{4,0},{8,12},{12,8},{16,20},{20,16},{24,28},{28,24},{1,5},{5... | collective-permute-start | bytes 1769480 | tf_op jit(solution)/shard_map/ppermute | solution.py:224
  67.7 11.9 %collective-permute-start.11 = (bf16[128,768]{1,0:T(8,128)(2,1)S(1)}, bf16[128,768]{1,0:T(8,128)(2,1)S(1)}, u32[]{:S(2)}, u32[]{:S(2)}) collective-permute-start(bf16[128,768]{1,0:T(8,128)(2,1)S(1)} %get-tuple-element.200), channel_id=1, source_target_pairs={{0,1},{1,2},{2,3},{3,0},{4,5},{5,6},{6,7},{7,4},{8,9},{9,10},{10,1... | collective-permute-start | bytes 589832 | tf_op jit(solution)/shard_map/ppermute | solution.py:1067
  71.5 13.5 %collective-permute-start.12 = (bf16[128,768]{1,0:T(8,128)(2,1)S(1)}, bf16[128,768]{1,0:T(8,128)(2,1)S(1)}, u32[]{:S(2)}, u32[]{:S(2)}) collective-permute-start(bf16[128,768]{1,0:T(8,128)(2,1)S(1)} %get-tuple-element.201), channel_id=1, source_target_pairs={{0,2},{1,3},{2,0},{3,1},{4,6},{5,7},{6,4},{7,5},{8,10},{9,11},{10,... | collective-permute-start | bytes 589832 | tf_op jit(solution)/shard_map/ppermute | solution.py:1067
  73.6 19.5 %collective-permute-start.14 = (bf16[192,768]{1,0:T(8,128)(2,1)S(1)}, bf16[192,768]{1,0:T(8,128)(2,1)S(1)}, u32[]{:S(2)}, u32[]{:S(2)}) collective-permute-start(bf16[192,768]{1,0:T(8,128)(2,1)S(1)} %get-tuple-element.209.refs_0_), channel_id=1, source_target_pairs={{0,8},{4,12},{8,0},{12,4},{16,24},{20,28},{24,16},{28,20},{1,9},{5... | collective-permute-start | bytes 884744 | tf_op jit(solution)/shard_map/ppermute | solution.py:224
  75.2 21.2 %collective-permute-start.15 = (bf16[192,768]{1,0:T(8,128)(2,1)S(1)}, bf16[192,768]{1,0:T(8,128)(2,1)S(1)}, u32[]{:S(2)}, u32[]{:S(2)}) collective-permute-start(bf16[192,768]{1,0:T(8,128)(2,1)S(1)} %get-tuple-element.210.refs_1_), channel_id=1, source_target_pairs={{0,16},{4,20},{8,24},{12,28},{16,0},{20,4},{24,8},{28,12},{1,17},{... | collective-permute-start | bytes 884744 | tf_op jit(solution)/shard_map/ppermute | solution.py:224
  76.7 10.0 %collective-permute-start.13 = (bf16[128,768]{1,0:T(8,128)(2,1)S(1)}, bf16[128,768]{1,0:T(8,128)(2,1)S(1)}, u32[]{:S(2)}, u32[]{:S(2)}) collective-permute-start(bf16[128,768]{1,0:T(8,128)(2,1)S(1)} %get-tuple-element.202), channel_id=1, source_target_pairs={{0,3},{1,0},{2,1},{3,2},{4,7},{5,4},{6,5},{7,6},{8,11},{9,8},{10,9... | collective-permute-start | bytes 589832 | tf_op jit(solution)/shard_map/ppermute | solution.py:1067
  79.6 17.3 %collective-permute-start.16 = (bf16[192,768]{1,0:T(8,128)(2,1)S(1)}, bf16[192,768]{1,0:T(8,128)(2,1)S(1)}, u32[]{:S(2)}, u32[]{:S(2)}) collective-permute-start(bf16[192,768]{1,0:T(8,128)(2,1)S(1)} %get-tuple-element.211.refs_2_), channel_id=1, source_target_pairs={{0,8},{4,12},{8,0},{12,4},{16,24},{20,28},{24,16},{28,20},{1,9},{5... | collective-permute-start | bytes 884744 | tf_op jit(solution)/shard_map/ppermute | solution.py:224
  85.0 11.9 %collective-permute-start.17 = (bf16[192,768]{1,0:T(8,128)(2,1)S(1)}, bf16[192,768]{1,0:T(8,128)(2,1)S(1)}, u32[]{:S(2)}, u32[]{:S(2)}) collective-permute-start(bf16[192,768]{1,0:T(8,128)(2,1)S(1)} %get-tuple-element.212.refs_3_), channel_id=1, source_target_pairs={{0,16},{4,20},{8,24},{12,28},{16,0},{20,4},{24,8},{28,12},{1,17},{... | collective-permute-start | bytes 884744 | tf_op jit(solution)/shard_map/ppermute | solution.py:224
  87.2 19.0 %collective-permute-start.18 = (bf16[128,768]{1,0:T(8,128)(2,1)S(1)}, bf16[128,768]{1,0:T(8,128)(2,1)S(1)}, u32[]{:S(2)}, u32[]{:S(2)}) collective-permute-start(bf16[128,768]{1,0:T(8,128)(2,1)S(1)} %get-tuple-element.216), channel_id=1, source_target_pairs={{0,2},{1,3},{2,0},{3,1},{4,6},{5,7},{6,4},{7,5},{8,10},{9,11},{10,... | collective-permute-start | bytes 589832 | tf_op jit(solution)/shard_map/ppermute | solution.py:1067
  93.1 13.0 %collective-permute-start.19 = (bf16[128,768]{1,0:T(8,128)(2,1)S(1)}, bf16[128,768]{1,0:T(8,128)(2,1)S(1)}, u32[]{:S(2)}, u32[]{:S(2)}) collective-permute-start(bf16[128,768]{1,0:T(8,128)(2,1)S(1)} %get-tuple-element.217), channel_id=1, source_target_pairs={{0,1},{1,2},{2,3},{3,0},{4,5},{5,6},{6,7},{7,4},{8,9},{9,10},{10,1... | collective-permute-start | bytes 589832 | tf_op jit(solution)/shard_map/ppermute | solution.py:1067
  96.4 10.4 %collective-permute-start.20 = (bf16[128,768]{1,0:T(8,128)(2,1)S(1)}, bf16[128,768]{1,0:T(8,128)(2,1)S(1)}, u32[]{:S(2)}, u32[]{:S(2)}) collective-permute-start(bf16[128,768]{1,0:T(8,128)(2,1)S(1)} %get-tuple-element.218), channel_id=1, source_target_pairs={{0,3},{1,0},{2,1},{3,2},{4,7},{5,4},{6,5},{7,6},{8,11},{9,8},{10,9... | collective-permute-start | bytes 589832 | tf_op jit(solution)/shard_map/ppermute | solution.py:1067
  97.2 18.6 %collective-permute-start.21 = (bf16[384,768]{1,0:T(8,128)(2,1)S(1)}, bf16[384,768]{1,0:T(8,128)(2,1)S(1)}, u32[]{:S(2)}, u32[]{:S(2)}) collective-permute-start(bf16[384,768]{1,0:T(8,128)(2,1)S(1)} %get-tuple-element.228.own_a), channel_id=1, source_target_pairs={{0,16},{4,20},{8,24},{12,28},{16,0},{20,4},{24,8},{28,12},{1,17},{... | collective-permute-start | bytes 1769480 | tf_op jit(solution)/shard_map/ppermute | solution.py:224
  97.8 18.1 %collective-permute-start.22 = (bf16[384,768]{1,0:T(8,128)(2,1)S(1)}, bf16[384,768]{1,0:T(8,128)(2,1)S(1)}, u32[]{:S(2)}, u32[]{:S(2)}) collective-permute-start(bf16[384,768]{1,0:T(8,128)(2,1)S(1)} %get-tuple-element.229.own_b), channel_id=1, source_target_pairs={{0,8},{4,12},{8,0},{12,4},{16,24},{20,28},{24,16},{28,20},{1,9},{5... | collective-permute-start | bytes 1769480 | tf_op jit(solution)/shard_map/ppermute | solution.py:224
  115.8 5.8 %copy-start.5 = (f32[2,768]{1,0:T(2,128)S(1)}, f32[2,768]{1,0:T(2,128)}, u32[]{:S(2)}) copy-start(f32[2,768]{1,0:T(2,128)} %wide_old.1) | copy-start | bytes 18436
  116.2 5.5 %collective-permute-start.24 = (bf16[768,768]{1,0:T(8,128)(2,1)S(1)}, bf16[768,768]{1,0:T(8,128)(2,1)S(1)}, u32[]{:S(2)}, u32[]{:S(2)}) collective-permute-start(bf16[768,768]{1,0:T(8,128)(2,1)S(1)} %fold_feed_last.1.mine), channel_id=1, source_target_pairs={{0,4},{4,0},{8,12},{12,8},{16,20},{20,16},{24,28},{28,24},{1,5},{5... | collective-permute-start | bytes 3538952 | tf_op jit(solution)/shard_map/ppermute | solution.py:224
  116.2 3.7 %collective-permute-start.23 = (bf16[400,768]{1,0:T(8,128)(2,1)S(1)}, bf16[400,768]{1,0:T(8,128)(2,1)S(1)}, u32[]{:S(2)}, u32[]{:S(2)}) collective-permute-start(bf16[400,768]{1,0:T(8,128)(2,1)S(1)} %get-tuple-element.230), channel_id=1, source_target_pairs={{0,4},{4,0},{8,12},{12,8},{16,20},{20,16},{24,28},{28,24},{1,5},{5... | collective-permute-start | bytes 1843208 | tf_op jit(solution)/shard_map/ppermute | solution.py:224
  120.1 9.8 %collective-permute-start.25 = (bf16[208,768]{1,0:T(8,128)(2,1)S(1)}, bf16[208,768]{1,0:T(8,128)(2,1)S(1)}, u32[]{:S(2)}, u32[]{:S(2)}) collective-permute-start(bf16[208,768]{1,0:T(8,128)(2,1)S(1)} %get-tuple-element.236.own_a), channel_id=1, source_target_pairs={{0,8},{4,12},{8,0},{12,4},{16,24},{20,28},{24,16},{28,20},{1,9},{5... | collective-permute-start | bytes 958472 | tf_op jit(solution)/shard_map/ppermute | solution.py:224
  121.2 8.8 %collective-permute-start.26 = (bf16[192,768]{1,0:T(8,128)(2,1)S(1)}, bf16[192,768]{1,0:T(8,128)(2,1)S(1)}, u32[]{:S(2)}, u32[]{:S(2)}) collective-permute-start(bf16[192,768]{1,0:T(8,128)(2,1)S(1)} %get-tuple-element.237.own_b), channel_id=1, source_target_pairs={{0,16},{4,20},{8,24},{12,28},{16,0},{20,4},{24,8},{28,12},{1,17},{... | collective-permute-start | bytes 884744 | tf_op jit(solution)/shard_map/ppermute | solution.py:224
  130.1 8.9 %collective-permute-start.27 = (bf16[208,768]{1,0:T(8,128)(2,1)S(1)}, bf16[208,768]{1,0:T(8,128)(2,1)S(1)}, u32[]{:S(2)}, u32[]{:S(2)}) collective-permute-start(bf16[208,768]{1,0:T(8,128)(2,1)S(1)} %get-tuple-element.246.own_a), channel_id=1, source_target_pairs={{0,16},{4,20},{8,24},{12,28},{16,0},{20,4},{24,8},{28,12},{1,17},{... | collective-permute-start | bytes 958472 | tf_op jit(solution)/shard_map/ppermute | solution.py:224
  130.9 7.7 %collective-permute-start.28 = (bf16[192,768]{1,0:T(8,128)(2,1)S(1)}, bf16[192,768]{1,0:T(8,128)(2,1)S(1)}, u32[]{:S(2)}, u32[]{:S(2)}) collective-permute-start(bf16[192,768]{1,0:T(8,128)(2,1)S(1)} %get-tuple-element.247.own_b), channel_id=1, source_target_pairs={{0,8},{4,12},{8,0},{12,4},{16,24},{20,28},{24,16},{28,20},{1,9},{5... | collective-permute-start | bytes 884744 | tf_op jit(solution)/shard_map/ppermute | solution.py:224
  131.9 9.3 %copy-start.2 = (f32[4,2,768]{2,1,0:T(2,128)S(1)}, f32[4,2,768]{2,1,0:T(2,128)}, u32[]{:S(2)}) copy-start(f32[4,2,768]{2,1,0:T(2,128)} %stats.3) | copy-start | bytes 73732
  139.0 13.5 %copy-start.3 = (f32[4,768]{1,0:T(4,128)S(1)}, f32[4,768]{1,0:T(4,128)}, u32[]{:S(2)}) copy-start(f32[4,768]{1,0:T(4,128)} %vec_moment.1) | copy-start | bytes 36868
  139.0 13.5 %copy-start.4 = (f32[2,768]{1,0:T(2,128)S(1)}, f32[2,768]{1,0:T(2,128)}, u32[]{:S(2)}) copy-start(f32[2,768]{1,0:T(2,128)} %narrow_old.1) | copy-start | bytes 18436
  139.1 2.1 %collective-permute-start.29 = (bf16[384,768]{1,0:T(8,128)(2,1)S(1)}, bf16[384,768]{1,0:T(8,128)(2,1)S(1)}, u32[]{:S(2)}, u32[]{:S(2)}) collective-permute-start(bf16[384,768]{1,0:T(8,128)(2,1)S(1)} %get-tuple-element.249.even), channel_id=1, source_target_pairs={{0,4},{4,0},{8,12},{12,8},{16,20},{20,16},{24,28},{28,24},{1,5},{5... | collective-permute-start | bytes 1769480 | tf_op jit(solution)/shard_map/ppermute | solution.py:224
  142.8 7.6 %collective-permute-start.32 = (bf16[32,768]{1,0:T(8,128)(2,1)S(1)}, bf16[32,768]{1,0:T(8,128)(2,1)S(1)}, u32[]{:S(2)}, u32[]{:S(2)}) collective-permute-start(bf16[32,768]{1,0:T(8,128)(2,1)S(1)} %get-tuple-element.263.share), channel_id=1, source_target_pairs={{0,3},{1,2},{2,1},{3,0},{4,7},{5,6},{6,5},{7,4},{8,11},{9,10},{10,... | collective-permute-start | bytes 147464 | tf_op jit(solution)/shard_map/ppermute | solution.py:1067
  146.6 5.0 %collective-permute-start.31 = (bf16[32,768]{1,0:T(8,128)(2,1)S(1)}, bf16[32,768]{1,0:T(8,128)(2,1)S(1)}, u32[]{:S(2)}, u32[]{:S(2)}) collective-permute-start(bf16[32,768]{1,0:T(8,128)(2,1)S(1)} %get-tuple-element.263.share), channel_id=1, source_target_pairs={{0,2},{1,3},{2,0},{3,1},{4,6},{5,7},{6,4},{7,5},{8,10},{9,11},{10,... | collective-permute-start | bytes 147464 | tf_op jit(solution)/shard_map/ppermute | solution.py:1067
  148.4 4.1 %collective-permute-start.30 = (bf16[32,768]{1,0:T(8,128)(2,1)S(1)}, bf16[32,768]{1,0:T(8,128)(2,1)S(1)}, u32[]{:S(2)}, u32[]{:S(2)}) collective-permute-start(bf16[32,768]{1,0:T(8,128)(2,1)S(1)} %get-tuple-element.263.share), channel_id=1, source_target_pairs={{0,1},{1,0},{2,3},{3,2},{4,5},{5,4},{6,7},{7,6},{8,9},{9,8},{10,11... | collective-permute-start | bytes 147464 | tf_op jit(solution)/shard_map/ppermute | solution.py:1067
where the time goes:
time: 158 us
  starting transfers between devices  58.6 us (37%)
  Pallas kernels  53 us (34%)
  waiting for transfers between devices  44.2 us (28%)
    ppermute x18, starting transfers between devices, exchange(): lax.ppermute(part, 'mp', [(i, target(i, step, ranks)) for i in range(rank...  45.7 us
    ppermute x18, waiting for transfers between devices, exchange(): lax.ppermute(part, 'mp', [(i, target(i, step, ranks)) for i in range(rank...  31.9 us
    ppermute x15, starting transfers between devices, across(): return lax.ppermute(block, 'dp', [(i, i ^ bit) for i in range(STAGED)])  13 us
    ppermute x15, waiting for transfers between devices, across(): return lax.ppermute(block, 'dp', [(i, i ^ bit) for i in range(STAGED)])  12.3 us
    pallas_call x1, Pallas kernels, prepare(): pl.pallas_call(functools.partial(prepare_kernel, seqs, tokens_pack), grid...  8.83 us
    pallas_call x1, Pallas kernels, forward(): pl.pallas_call(functools.partial(forward_kernel, local), out_shape=[near(...  8.14 us
    pallas_call x1, Pallas kernels, update(): pl.pallas_call(functools.partial(update_kernel, hidden_all), in_specs=[pl...  4.96 us
    pallas_call x1, Pallas kernels, mix_second(): pl.pallas_call(mix_second_kernel, out_shape=[near((tokens, width), bf16)]...  4.66 us
  transfers between devices with their start and end apart: 33, of which 15 were waited for; matrix products, arithmetic and copies ran while one was open for 0% of the time, Pallas kernels for 22%

commit v1 on v0

--- a/solution.py
+++ b/solution.py
@@ -1159,10 +1159,10 @@
         *d_mix, attn_low, d_resid, attn_weight, up_weight, down_weight, own_width
     )
     if staged:
-        attn_a, feed_shares = lax.optimization_barrier((attn_a, feed_shares))
+        attn_a, tokens_grad = lax.optimization_barrier((attn_a, tokens_grad))
         vec_part, attn_a, attn_b = fold_second(attn_a, got_a, attn_b, got_b, vec_part)
         got_a, got_b = across(attn_a, 4), across(attn_b, 2)
-        attn_a, tokens_grad = lax.optimization_barrier((attn_a, tokens_grad))
+        attn_a, feed_shares = lax.optimization_barrier((attn_a, feed_shares))
         vec_part, attn_even = fold_last(attn_a, got_a, attn_b, got_b, vec_part)
         attn_odd = across(attn_even, 1)
     attn_near, rows_near, shares = attn_stats_call(attn_even, attn_odd, vec_part, attn_stats, feed_shares, own_width)

time: 158 us -> 156 us (0.987)
  waiting for transfers between devices: 44.2 us -> 42.3 us
    ppermute x15, waiting for transfers between devices: 12.3 us -> 10.3 us  [across(): return lax.ppermute(block, 'dp', [(i, i ^ bit) for i in range(STAGED)])]
where the time goes in v1:
time: 156 us
  starting transfers between devices  58.4 us (37%)
  Pallas kernels  53.3 us (34%)
  waiting for transfers between devices  42.3 us (27%)
    ppermute x18, starting transfers between devices, exchange(): lax.ppermute(part, 'mp', [(i, target(i, step, ranks)) for i in range(rank...  45.7 us
    ppermute x18, waiting for transfers between devices, exchange(): lax.ppermute(part, 'mp', [(i, target(i, step, ranks)) for i in range(rank...  31.9 us
    ppermute x15, starting transfers between devices, across(): return lax.ppermute(block, 'dp', [(i, i ^ bit) for i in range(STAGED)])  12.7 us
    ppermute x15, waiting for transfers between devices, across(): return lax.ppermute(block, 'dp', [(i, i ^ bit) for i in range(STAGED)])  10.3 us
    pallas_call x1, Pallas kernels, prepare(): pl.pallas_call(functools.partial(prepare_kernel, seqs, tokens_pack), grid...  8.83 us
    pallas_call x1, Pallas kernels, forward(): pl.pallas_call(functools.partial(forward_kernel, local), out_shape=[near(...  8.15 us
    pallas_call x1, Pallas kernels, update(): pl.pallas_call(functools.partial(update_kernel, hidden_all), in_specs=[pl...  4.96 us
    pallas_call x1, Pallas kernels, mix_second(): pl.pallas_call(mix_second_kernel, out_shape=[near((tokens, width), bf16)]...  4.69 us
  transfers between devices with their start and end apart: 33, of which 15 were waited for; matrix products, arithmetic and copies ran while one was open for 0% of the time, Pallas kernels for 22%

profile of v1, /device:TPU:0, one launch (start us, length us, event | category | flops | bytes accessed | tf_op | source)
XLA Modules:
  0.0 155.7 jit_solution(12134199531164630615)
XLA Ops:
  0.7 3.1 %collective-permute-start.1 = (bf16[128,768]{1,0:T(8,128)(2,1)}, bf16[128,768]{1,0:T(8,128)(2,1)S(1)}, u32[]{:S(2)}, u32[]{:S(2)}) collective-permute-start(bf16[128,768]{1,0:T(8,128)(2,1)} %x0.1), channel_id=1, source_target_pairs={{0,1},{1,0},{2,3},{3,2},{4,5},{5,4},{6,7},{7,6},{8,9},{9,8},{10,11... | collective-permute-start | bytes 589832 | tf_op jit(solution)/shard_map/ppermute | solution.py:1067
  3.8 2.6 %collective-permute-start = (bf16[128,768]{1,0:T(8,128)(2,1)}, bf16[128,768]{1,0:T(8,128)(2,1)S(1)}, u32[]{:S(2)}, u32[]{:S(2)}) collective-permute-start(bf16[128,768]{1,0:T(8,128)(2,1)} %x0.1), channel_id=1, source_target_pairs={{0,2},{1,3},{2,0},{3,1},{4,6},{5,7},{6,4},{7,5},{8,10},{9,11},{10,... | collective-permute-start | bytes 589832 | tf_op jit(solution)/shard_map/ppermute | solution.py:1067
  6.3 0.7 copy-done.6
  7.0 8.8 %prepare.1 = (bf16[4,768,768]{2,1,0:T(8,128)(2,1)S(1)}, bf16[768,768]{1,0:T(8,128)(2,1)S(1)}, bf16[768,768]{1,0:T(8,128)(2,1)S(1)}, f32[512,512]{1,0:T(8,128)S(1...) custom-call(s32[1,8]{1,0:T(1,128)S(1)} %copy-done.6, f32[4,768,768]{2,1,0:T(8,128)} %attn_weight.1, ...), custom_call_target="tpu_custom_call" | custom-call | flops 10000000 | bytes 22000000 | tf_op jit(solution)/shard_map/prepare/pallas_call | solution.py:275
  15.9 5.3 %collective-permute-done.x1 = bf16[128,768]{1,0:T(8,128)(2,1)S(1)} collective-permute-done((bf16[128,768]{1,0:T(8,128)(2,1)}, bf16[128,768]{1,0:T(8,128)(2,1)S(1)}, u32[]{:S(2)}, u32[]{:S(2)}) %collective-permute-start) | collective-permute-done | bytes 196640 | tf_op jit(solution)/shard_map/ppermute | solution.py:1067
  21.1 8.1 %forward.1 = (bf16[512,768]{1,0:T(8,128)(2,1)S(1)}, bf16[512,768]{1,0:T(8,128)(2,1)S(1)}, bf16[512,768]{1,0:T(8,128)(2,1)S(1)}, bf16[512,768]{1,0:T(8,128)(2,1)S...) custom-call(bf16[128,768]{1,0:T(8,128)(2,1)S(1)} %copy-done.7, ...), custom_call_target="tpu_custom_call" | custom-call | flops 8000000000 | bytes 20000000 | tf_op jit(solution)/shard_map/forward/pallas_call | solution.py:424
  29.3 3.4 %collective-permute-start.3 = (bf16[128,768]{1,0:T(8,128)(2,1)S(1)}, bf16[128,768]{1,0:T(8,128)(2,1)S(1)}, u32[]{:S(2)}, u32[]{:S(2)}) collective-permute-start(bf16[128,768]{1,0:T(8,128)(2,1)S(1)} %get-tuple-element.154), channel_id=1, source_target_pairs={{0,1},{1,2},{2,3},{3,0},{4,5},{5,6},{6,7},{7,4},{8,9},{9,10},{10,1... | collective-permute-start | bytes 589832 | tf_op jit(solution)/shard_map/ppermute | solution.py:1067
  32.7 1.1 collective-permute-start.4
  33.8 2.8 %collective-permute-start.5 = (bf16[128,768]{1,0:T(8,128)(2,1)S(1)}, bf16[128,768]{1,0:T(8,128)(2,1)S(1)}, u32[]{:S(2)}, u32[]{:S(2)}) collective-permute-start(bf16[128,768]{1,0:T(8,128)(2,1)S(1)} %get-tuple-element.156), channel_id=1, source_target_pairs={{0,3},{1,0},{2,1},{3,2},{4,7},{5,4},{6,5},{7,6},{8,11},{9,8},{10,9... | collective-permute-start | bytes 589832 | tf_op jit(solution)/shard_map/ppermute | solution.py:1067
  36.6 4.3 %slopes.1 = (bf16[6144,512]{1,0:T(8,128)(2,1)S(1)}, bf16[512,768]{1,0:T(8,128)(2,1)S(1)}, bf16[512,768]{1,0:T(8,128)(2,1)S(1)}, f32[512,768]{1,0:T(8,128)S(1)}) custom-call(bf16[512,768]{1,0:T(8,128)(2,1)S(1)} %get-tuple-element.158.query_feat.refs_10_.refs_11_, bf16[512,768]{1,0:T(8,128)(2,1)S(1)} %get-tuple-element.159.key_feat.refs_11_.refs_12_, ...), custom_call_target="tpu_custom_call" | custom-call | tf_op jit(solution)/shard_map/slopes/pallas_call | solution.py:466
  40.9 4.4 %collective-permute-done.4.refs_2_ = bf16[128,768]{1,0:T(8,128)(2,1)S(1)} collective-permute-done((bf16[128,768]{1,0:T(8,128)(2,1)S(1)}, bf16[128,768]{1,0:T(8,128)(2,1)S(1)}, u32[]{:S(2)}, u32[]{:S(2)}) %collective-permute-start.4) | collective-permute-done | bytes 196640 | tf_op jit(solution)/shard_map/ppermute | solution.py:1067
  45.3 0.4 middle.1
  45.8 4.5 %collective-permute-start.6 = (bf16[128,768]{1,0:T(8,128)(2,1)S(1)}, bf16[128,768]{1,0:T(8,128)(2,1)S(1)}, u32[]{:S(2)}, u32[]{:S(2)}) collective-permute-start(bf16[128,768]{1,0:T(8,128)(2,1)S(1)} %get-tuple-element.179), channel_id=1, source_target_pairs={{0,2},{1,3},{2,0},{3,1},{4,6},{5,7},{6,4},{7,5},{8,10},{9,11},{10,... | collective-permute-start | bytes 589832 | tf_op jit(solution)/shard_map/ppermute | solution.py:1067
  50.2 3.5 %collective-permute-start.7 = (bf16[128,768]{1,0:T(8,128)(2,1)S(1)}, bf16[128,768]{1,0:T(8,128)(2,1)S(1)}, u32[]{:S(2)}, u32[]{:S(2)}) collective-permute-start(bf16[128,768]{1,0:T(8,128)(2,1)S(1)} %get-tuple-element.180), channel_id=1, source_target_pairs={{0,1},{1,2},{2,3},{3,0},{4,5},{5,6},{6,7},{7,4},{8,9},{9,10},{10,1... | collective-permute-start | bytes 589832 | tf_op jit(solution)/shard_map/ppermute | solution.py:1067
  53.8 0.3 collective-permute-start.8
  54.1 1.2 own_columns.1
  55.3 8.6 %collective-permute-done.6.refs_1_ = bf16[128,768]{1,0:T(8,128)(2,1)S(1)} collective-permute-done((bf16[128,768]{1,0:T(8,128)(2,1)S(1)}, bf16[128,768]{1,0:T(8,128)(2,1)S(1)}, u32[]{:S(2)}, u32[]{:S(2)}) %collective-permute-start.6) | collective-permute-done | bytes 196640 | tf_op jit(solution)/shard_map/ppermute | solution.py:1067
  63.8 0.2 collective-permute-done.8.refs_3_
  64.1 1.7 %feed_back.1 = (bf16[512,768]{1,0:T(8,128)(2,1)S(1)}, bf16[512,768]{1,0:T(8,128)(2,1)S(1)}, f32[128,768]{1,0:T(8,128)S(1)}, bf16[128,768]{1,0:T(8,128)(2,1)S(1)}...) custom-call(bf16[128,768]{1,0:T(8,128)(2,1)S(1)} %get-tuple-element.178.refs_0_, ...), custom_call_target="tpu_custom_call" | custom-call | flops 1200000000 | bytes 9000000 | tf_op jit(solution)/shard_map/feed_back/pallas_call | solution.py:524
  65.7 1.4 feed_grads.1
  67.2 0.5 collective-permute-start.10
  67.7 3.8 %collective-permute-start.11 = (bf16[128,768]{1,0:T(8,128)(2,1)S(1)}, bf16[128,768]{1,0:T(8,128)(2,1)S(1)}, u32[]{:S(2)}, u32[]{:S(2)}) collective-permute-start(bf16[128,768]{1,0:T(8,128)(2,1)S(1)} %get-tuple-element.200), channel_id=1, source_target_pairs={{0,1},{1,2},{2,3},{3,0},{4,5},{5,6},{6,7},{7,4},{8,9},{9,10},{10,1... | collective-permute-start | bytes 589832 | tf_op jit(solution)/shard_map/ppermute | solution.py:1067
  71.5 1.9 %collective-permute-start.12 = (bf16[128,768]{1,0:T(8,128)(2,1)S(1)}, bf16[128,768]{1,0:T(8,128)(2,1)S(1)}, u32[]{:S(2)}, u32[]{:S(2)}) collective-permute-start(bf16[128,768]{1,0:T(8,128)(2,1)S(1)} %get-tuple-element.201), channel_id=1, source_target_pairs={{0,2},{1,3},{2,0},{3,1},{4,6},{5,7},{6,4},{7,5},{8,10},{9,11},{10,... | collective-permute-start | bytes 589832 | tf_op jit(solution)/shard_map/ppermute | solution.py:1067
  73.6 1.5 collective-permute-start.14
  75.2 1.5 collective-permute-start.15
  76.7 2.9 %collective-permute-start.13 = (bf16[128,768]{1,0:T(8,128)(2,1)S(1)}, bf16[128,768]{1,0:T(8,128)(2,1)S(1)}, u32[]{:S(2)}, u32[]{:S(2)}) collective-permute-start(bf16[128,768]{1,0:T(8,128)(2,1)S(1)} %get-tuple-element.202), channel_id=1, source_target_pairs={{0,3},{1,0},{2,1},{3,2},{4,7},{5,4},{6,5},{7,6},{8,11},{9,8},{10,9... | collective-permute-start | bytes 589832 | tf_op jit(solution)/shard_map/ppermute | solution.py:1067
  79.6 0.5 collective-permute-start.16
  80.2 4.9 %collective-permute-done.12.refs_2_ = bf16[128,768]{1,0:T(8,128)(2,1)S(1)} collective-permute-done((bf16[128,768]{1,0:T(8,128)(2,1)S(1)}, bf16[128,768]{1,0:T(8,128)(2,1)S(1)}, u32[]{:S(2)}, u32[]{:S(2)}) %collective-permute-start.12) | collective-permute-done | bytes 196640 | tf_op jit(solution)/shard_map/ppermute | solution.py:1067
  85.0 1.5 collective-permute-start.17
  86.6 0.2 collective-permute-done.13.refs_3_
  86.7 0.4 first_back.1
  87.2 5.9 %collective-permute-start.18 = (bf16[128,768]{1,0:T(8,128)(2,1)S(1)}, bf16[128,768]{1,0:T(8,128)(2,1)S(1)}, u32[]{:S(2)}, u32[]{:S(2)}) collective-permute-start(bf16[128,768]{1,0:T(8,128)(2,1)S(1)} %get-tuple-element.216), channel_id=1, source_target_pairs={{0,2},{1,3},{2,0},{3,1},{4,6},{5,7},{6,4},{7,5},{8,10},{9,11},{10,... | collective-permute-start | bytes 589832 | tf_op jit(solution)/shard_map/ppermute | solution.py:1067
  93.1 3.3 %collective-permute-start.19 = (bf16[128,768]{1,0:T(8,128)(2,1)S(1)}, bf16[128,768]{1,0:T(8,128)(2,1)S(1)}, u32[]{:S(2)}, u32[]{:S(2)}) collective-permute-start(bf16[128,768]{1,0:T(8,128)(2,1)S(1)} %get-tuple-element.217), channel_id=1, source_target_pairs={{0,1},{1,2},{2,3},{3,0},{4,5},{5,6},{6,7},{7,4},{8,9},{9,10},{10,1... | collective-permute-start | bytes 589832 | tf_op jit(solution)/shard_map/ppermute | solution.py:1067
  96.4 0.5 collective-permute-start.20
  97.0 0.3 fold_feed.1
  97.2 0.6 collective-permute-start.21
  97.8 2.7 %collective-permute-start.22 = (bf16[384,768]{1,0:T(8,128)(2,1)S(1)}, bf16[384,768]{1,0:T(8,128)(2,1)S(1)}, u32[]{:S(2)}, u32[]{:S(2)}) collective-permute-start(bf16[384,768]{1,0:T(8,128)(2,1)S(1)} %get-tuple-element.229.own_b), channel_id=1, source_target_pairs={{0,8},{4,12},{8,0},{12,4},{16,24},{20,28},{24,16},{28,20},{1,9},{5... | collective-permute-start | bytes 1769480 | tf_op jit(solution)/shard_map/ppermute | solution.py:224
  100.5 5.7 %collective-permute-done.18.a1 = bf16[128,768]{1,0:T(8,128)(2,1)S(1)} collective-permute-done((bf16[128,768]{1,0:T(8,128)(2,1)S(1)}, bf16[128,768]{1,0:T(8,128)(2,1)S(1)}, u32[]{:S(2)}, u32[]{:S(2)}) %collective-permute-start.18) | collective-permute-done | bytes 196640 | tf_op jit(solution)/shard_map/ppermute | solution.py:1067
  106.1 0.7 collective-permute-done.20.a3
  106.8 4.3 %mix_first.1 = (bf16[512,768]{1,0:T(8,128)(2,1)S(1)}, bf16[512,768]{1,0:T(8,128)(2,1)S(1)}, bf16[512,768]{1,0:T(8,128)(2,1)S(1)}, bf16[512,384]{1,0:T(8,128)(2,1...) custom-call(bf16[128,768]{1,0:T(8,128)(2,1)S(1)} %get-tuple-element.215.a0, ...), custom_call_target="tpu_custom_call" | custom-call | flops 6000000000 | bytes 18000000 | tf_op jit(solution)/shard_map/mix_first/pallas_call | solution.py:691
  111.2 4.7 %mix_second.1 = (bf16[512,768]{1,0:T(8,128)(2,1)S(1)}, bf16[512,768]{1,0:T(8,128)(2,1)S(1)}, bf16[512,768]{1,0:T(8,128)(2,1)S(1)}, f32[8,768]{1,0:T(8,128)S(1)},...) custom-call(bf16[512,768]{1,0:T(8,128)(2,1)S(1)} %get-tuple-element.219.d_attn, ...), custom_call_target="tpu_custom_call" | custom-call | flops 6000000000 | bytes 18000000 | tf_op jit(solution)/shard_map/mix_second/pallas_call | solution.py:749
  115.9 0.3 fold_feed_last.1.mine
  116.3 0.5 collective-permute-start.26
  116.8 1.5 collective-permute-done.23.received
  118.4 1.1 collective-permute-start.24
  119.5 0.5 collective-permute-start.25
  120.0 4.6 %tokens_back.1 = (f32[128,768]{1,0:T(8,128)}, f32[4,192,768]{2,1,0:T(8,128)S(1)}, f32[768,768]{1,0:T(8,128)S(1)}, f32[768,768]{1,0:T(8,128)S(1)}) custom-call(bf16[512,768]{1,0:T(8,128)(2,1)S(1)} %get-tuple-element.233.d_query, bf16[512,768]{1,0:T(8,128)(2,1)S(1)} %get-tuple-element.234.d_key, bf16[512,768]{1,0:T(8,128)(2,1)S(1)} %get-tuple-element.235.d_value, ...), custom_call_target="tpu_custom_call" | custom-call | tf_op jit(solution)/shard_map/tokens_back/pallas_call | solution.py:790
  124.6 3.7 %collective-permute-done.25.got_b = bf16[192,768]{1,0:T(8,128)(2,1)S(1)} collective-permute-done((bf16[192,768]{1,0:T(8,128)(2,1)S(1)}, bf16[192,768]{1,0:T(8,128)(2,1)S(1)}, u32[]{:S(2)}, u32[]{:S(2)}) %collective-permute-start.25) | collective-permute-done | bytes 294944 | tf_op jit(solution)/shard_map/ppermute | solution.py:224
  128.3 0.1 fold_second.1
  128.4 0.6 collective-permute-start.27
  129.0 1.0 collective-permute-start.28
  130.0 3.9 %feed_stats.1 = (f32[768,768]{1,0:T(8,128)}, f32[768,768]{1,0:T(8,128)}, f32[2,768]{1,0:T(2,128)}, f32[1536,768]{1,0:T(8,128)S(1)}, f32[2,768]{1,0:T(2,128)S(1)}, /*index=5*/f32[8,768]{1,0:T(8,128)S(1)}) custom-call(bf16[768,768]{1,0:T(8,128)(2,1)S(1)} %fold_feed_last.1.mine, bf16[768,768]{1,0:T(8,128)(2,1)S(1)} %collective-permute-done.26.other, ...), custom_call_target="tpu_custom_call" | custom-call | tf_op jit(solution)/shard_map/feed_stats/pallas_call | solution.py:916
  134.0 2.8 %collective-permute-done.28.got_b = bf16[192,768]{1,0:T(8,128)(2,1)S(1)} collective-permute-done((bf16[192,768]{1,0:T(8,128)(2,1)S(1)}, bf16[192,768]{1,0:T(8,128)(2,1)S(1)}, u32[]{:S(2)}, u32[]{:S(2)}) %collective-permute-start.28) | collective-permute-done | bytes 294944 | tf_op jit(solution)/shard_map/ppermute | solution.py:224
  136.7 0.3 collective-permute-done.27.got_a
  137.0 0.1 fold_last.1
  137.3 2.0 %collective-permute-done.29.odd = bf16[384,768]{1,0:T(8,128)(2,1)S(1)} collective-permute-done((bf16[384,768]{1,0:T(8,128)(2,1)S(1)}, bf16[384,768]{1,0:T(8,128)(2,1)S(1)}, u32[]{:S(2)}, u32[]{:S(2)}) %collective-permute-start.29) | collective-permute-done | bytes 589856 | tf_op jit(solution)/shard_map/ppermute | solution.py:224
  139.3 1.7 %attn_stats.1 = (f32[768,768]{1,0:T(8,128)S(1)}, f32[4,192]{1,0:T(4,128)S(1)}, bf16[32,768]{1,0:T(8,128)(2,1)S(1)}) custom-call(bf16[384,768]{1,0:T(8,128)(2,1)S(1)} %get-tuple-element.249.even, bf16[384,768]{1,0:T(8,128)(2,1)S(1)} %collective-permute-done.29.odd, f32[8,768]{1,0:T(8,128)S(1)} %get-tuple-element.250.vec, f32[4,2,768]{2,1,0:T(2,128)S(1)} %copy-done.2, ...), custom_call_target="tpu_custom_call" | custom-call | tf_op jit(solution)/shard_map/attn_stats/pallas_call | solution.py:858
  140.9 3.8 %collective-permute-start.32 = (bf16[32,768]{1,0:T(8,128)(2,1)S(1)}, bf16[32,768]{1,0:T(8,128)(2,1)S(1)}, u32[]{:S(2)}, u32[]{:S(2)}) collective-permute-start(bf16[32,768]{1,0:T(8,128)(2,1)S(1)} %get-tuple-element.263.share), channel_id=1, source_target_pairs={{0,3},{1,2},{2,1},{3,0},{4,7},{5,6},{6,5},{7,4},{8,11},{9,10},{10,... | collective-permute-start | bytes 147464 | tf_op jit(solution)/shard_map/ppermute | solution.py:1067
  144.7 1.8 %collective-permute-start.31 = (bf16[32,768]{1,0:T(8,128)(2,1)S(1)}, bf16[32,768]{1,0:T(8,128)(2,1)S(1)}, u32[]{:S(2)}, u32[]{:S(2)}) collective-permute-start(bf16[32,768]{1,0:T(8,128)(2,1)S(1)} %get-tuple-element.263.share), channel_id=1, source_target_pairs={{0,2},{1,3},{2,0},{3,1},{4,6},{5,7},{6,4},{7,5},{8,10},{9,11},{10,... | collective-permute-start | bytes 147464 | tf_op jit(solution)/shard_map/ppermute | solution.py:1067
  146.4 0.5 collective-permute-start.30
  146.9 1.6 %attn_out.1 = (f32[4,192,768]{2,1,0:T(8,128)}, f32[4,192]{1,0:T(4,128)}) custom-call(f32[768,768]{1,0:T(8,128)S(1)} %get-tuple-element.257.total.attn_grad, f32[4,192]{1,0:T(4,128)S(1)} %get-tuple-element.253.rows.attn_rows), custom_call_target="tpu_custom_call" | custom-call | tf_op jit(solution)/shard_map/attn_out/pallas_call | solution.py:876
  148.5 1.2 collective-permute-done.31.share2
  149.7 0.8 collective-permute-done.30.share1
  150.5 5.0 %update.1 = (f32[4,192,768]{2,1,0:T(8,128)}, bf16[4,192,768]{2,1,0:T(8,128)(2,1)}, f32[768,768]{1,0:T(8,128)}, bf16[768,768]{1,0:T(8,128)(2,1)}, f32[768,768]{1,...) custom-call(f32[768,768]{1,0:T(8,128)S(1)} %get-tuple-element.257.to, ...), custom_call_target="tpu_custom_call" | custom-call | tf_op jit(solution)/shard_map/update/pallas_call | solution.py:1048
  (40 shorter events, 0.6 us)
Async XLA Ops:
  0.7 20.5 %copy-start.1 = (f32[4,768]{1,0:T(4,128)S(1)}, f32[4,768]{1,0:T(4,128)}, u32[]{:S(2)}) copy-start(f32[4,768]{1,0:T(4,128)} %vec.3) | copy-start | bytes 36868
  0.7 15.2 %collective-permute-start.1 = (bf16[128,768]{1,0:T(8,128)(2,1)}, bf16[128,768]{1,0:T(8,128)(2,1)S(1)}, u32[]{:S(2)}, u32[]{:S(2)}) collective-permute-start(bf16[128,768]{1,0:T(8,128)(2,1)} %x0.1), channel_id=1, source_target_pairs={{0,1},{1,0},{2,3},{3,2},{4,5},{5,4},{6,7},{7,6},{8,9},{9,8},{10,11... | collective-permute-start | bytes 589832 | tf_op jit(solution)/shard_map/ppermute | solution.py:1067
  3.8 17.4 %collective-permute-start = (bf16[128,768]{1,0:T(8,128)(2,1)}, bf16[128,768]{1,0:T(8,128)(2,1)S(1)}, u32[]{:S(2)}, u32[]{:S(2)}) collective-permute-start(bf16[128,768]{1,0:T(8,128)(2,1)} %x0.1), channel_id=1, source_target_pairs={{0,2},{1,3},{2,0},{3,1},{4,6},{5,7},{6,4},{7,5},{8,10},{9,11},{10,... | collective-permute-start | bytes 589832 | tf_op jit(solution)/shard_map/ppermute | solution.py:1067
  6.3 14.8 %collective-permute-start.2 = (bf16[128,768]{1,0:T(8,128)(2,1)}, bf16[128,768]{1,0:T(8,128)(2,1)S(1)}, u32[]{:S(2)}, u32[]{:S(2)}) collective-permute-start(bf16[128,768]{1,0:T(8,128)(2,1)} %x0.1), channel_id=1, source_target_pairs={{0,3},{1,2},{2,1},{3,0},{4,7},{5,6},{6,5},{7,4},{8,11},{9,10},{10,... | collective-permute-start | bytes 589832 | tf_op jit(solution)/shard_map/ppermute | solution.py:1067
  6.3 0.7 copy-start.6
  7.0 14.1 %copy-start.7 = (bf16[128,768]{1,0:T(8,128)(2,1)S(1)}, bf16[128,768]{1,0:T(8,128)(2,1)}, u32[]{:S(2)}) copy-start(bf16[128,768]{1,0:T(8,128)(2,1)} %x0.1) | copy-start | bytes 589828
  29.3 16.1 %copy-start = (bf16[128,768]{1,0:T(8,128)(2,1)S(1)}, bf16[128,768]{1,0:T(8,128)(2,1)}, u32[]{:S(2)}) copy-start(bf16[128,768]{1,0:T(8,128)(2,1)} %refs_5_.1) | copy-start | bytes 589828
  29.3 11.6 %collective-permute-start.3 = (bf16[128,768]{1,0:T(8,128)(2,1)S(1)}, bf16[128,768]{1,0:T(8,128)(2,1)S(1)}, u32[]{:S(2)}, u32[]{:S(2)}) collective-permute-start(bf16[128,768]{1,0:T(8,128)(2,1)S(1)} %get-tuple-element.154), channel_id=1, source_target_pairs={{0,1},{1,2},{2,3},{3,0},{4,5},{5,6},{6,7},{7,4},{8,9},{9,10},{10,1... | collective-permute-start | bytes 589832 | tf_op jit(solution)/shard_map/ppermute | solution.py:1067
  32.7 12.6 %collective-permute-start.4 = (bf16[128,768]{1,0:T(8,128)(2,1)S(1)}, bf16[128,768]{1,0:T(8,128)(2,1)S(1)}, u32[]{:S(2)}, u32[]{:S(2)}) collective-permute-start(bf16[128,768]{1,0:T(8,128)(2,1)S(1)} %get-tuple-element.155), channel_id=1, source_target_pairs={{0,2},{1,3},{2,0},{3,1},{4,6},{5,7},{6,4},{7,5},{8,10},{9,11},{10,... | collective-permute-start | bytes 589832 | tf_op jit(solution)/shard_map/ppermute | solution.py:1067
  33.8 11.6 %collective-permute-start.5 = (bf16[128,768]{1,0:T(8,128)(2,1)S(1)}, bf16[128,768]{1,0:T(8,128)(2,1)S(1)}, u32[]{:S(2)}, u32[]{:S(2)}) collective-permute-start(bf16[128,768]{1,0:T(8,128)(2,1)S(1)} %get-tuple-element.156), channel_id=1, source_target_pairs={{0,3},{1,0},{2,1},{3,2},{4,7},{5,4},{6,5},{7,6},{8,11},{9,8},{10,9... | collective-permute-start | bytes 589832 | tf_op jit(solution)/shard_map/ppermute | solution.py:1067
  45.8 18.1 %collective-permute-start.6 = (bf16[128,768]{1,0:T(8,128)(2,1)S(1)}, bf16[128,768]{1,0:T(8,128)(2,1)S(1)}, u32[]{:S(2)}, u32[]{:S(2)}) collective-permute-start(bf16[128,768]{1,0:T(8,128)(2,1)S(1)} %get-tuple-element.179), channel_id=1, source_target_pairs={{0,2},{1,3},{2,0},{3,1},{4,6},{5,7},{6,4},{7,5},{8,10},{9,11},{10,... | collective-permute-start | bytes 589832 | tf_op jit(solution)/shard_map/ppermute | solution.py:1067
  50.2 13.6 %collective-permute-start.7 = (bf16[128,768]{1,0:T(8,128)(2,1)S(1)}, bf16[128,768]{1,0:T(8,128)(2,1)S(1)}, u32[]{:S(2)}, u32[]{:S(2)}) collective-permute-start(bf16[128,768]{1,0:T(8,128)(2,1)S(1)} %get-tuple-element.180), channel_id=1, source_target_pairs={{0,1},{1,2},{2,3},{3,0},{4,5},{5,6},{6,7},{7,4},{8,9},{9,10},{10,1... | collective-permute-start | bytes 589832 | tf_op jit(solution)/shard_map/ppermute | solution.py:1067
  53.8 10.3 %collective-permute-start.8 = (bf16[128,768]{1,0:T(8,128)(2,1)S(1)}, bf16[128,768]{1,0:T(8,128)(2,1)S(1)}, u32[]{:S(2)}, u32[]{:S(2)}) collective-permute-start(bf16[128,768]{1,0:T(8,128)(2,1)S(1)} %get-tuple-element.181), channel_id=1, source_target_pairs={{0,3},{1,0},{2,1},{3,2},{4,7},{5,4},{6,5},{7,6},{8,11},{9,8},{10,9... | collective-permute-start | bytes 589832 | tf_op jit(solution)/shard_map/ppermute | solution.py:1067
  67.2 6.2 %collective-permute-start.9 = (bf16[384,768]{1,0:T(8,128)(2,1)S(1)}, bf16[384,768]{1,0:T(8,128)(2,1)S(1)}, u32[]{:S(2)}, u32[]{:S(2)}) collective-permute-start(bf16[384,768]{1,0:T(8,128)(2,1)S(1)} %get-tuple-element.192), channel_id=1, source_target_pairs={{0,4},{4,0},{8,12},{12,8},{16,20},{20,16},{24,28},{28,24},{1,5},{5... | collective-permute-start | bytes 1769480 | tf_op jit(solution)/shard_map/ppermute | solution.py:224
  67.2 6.3 %collective-permute-start.10 = (bf16[384,768]{1,0:T(8,128)(2,1)S(1)}, bf16[384,768]{1,0:T(8,128)(2,1)S(1)}, u32[]{:S(2)}, u32[]{:S(2)}) collective-permute-start(bf16[384,768]{1,0:T(8,128)(2,1)S(1)} %get-tuple-element.196), channel_id=1, source_target_pairs={{0,4},{4,0},{8,12},{12,8},{16,20},{20,16},{24,28},{28,24},{1,5},{5... | collective-permute-start | bytes 1769480 | tf_op jit(solution)/shard_map/ppermute | solution.py:224
  67.7 11.9 %collective-permute-start.11 = (bf16[128,768]{1,0:T(8,128)(2,1)S(1)}, bf16[128,768]{1,0:T(8,128)(2,1)S(1)}, u32[]{:S(2)}, u32[]{:S(2)}) collective-permute-start(bf16[128,768]{1,0:T(8,128)(2,1)S(1)} %get-tuple-element.200), channel_id=1, source_target_pairs={{0,1},{1,2},{2,3},{3,0},{4,5},{5,6},{6,7},{7,4},{8,9},{9,10},{10,1... | collective-permute-start | bytes 589832 | tf_op jit(solution)/shard_map/ppermute | solution.py:1067
  71.5 13.5 %collective-permute-start.12 = (bf16[128,768]{1,0:T(8,128)(2,1)S(1)}, bf16[128,768]{1,0:T(8,128)(2,1)S(1)}, u32[]{:S(2)}, u32[]{:S(2)}) collective-permute-start(bf16[128,768]{1,0:T(8,128)(2,1)S(1)} %get-tuple-element.201), channel_id=1, source_target_pairs={{0,2},{1,3},{2,0},{3,1},{4,6},{5,7},{6,4},{7,5},{8,10},{9,11},{10,... | collective-permute-start | bytes 589832 | tf_op jit(solution)/shard_map/ppermute | solution.py:1067
  73.6 19.5 %collective-permute-start.14 = (bf16[192,768]{1,0:T(8,128)(2,1)S(1)}, bf16[192,768]{1,0:T(8,128)(2,1)S(1)}, u32[]{:S(2)}, u32[]{:S(2)}) collective-permute-start(bf16[192,768]{1,0:T(8,128)(2,1)S(1)} %get-tuple-element.209.refs_0_), channel_id=1, source_target_pairs={{0,8},{4,12},{8,0},{12,4},{16,24},{20,28},{24,16},{28,20},{1,9},{5... | collective-permute-start | bytes 884744 | tf_op jit(solution)/shard_map/ppermute | solution.py:224
  75.2 21.2 %collective-permute-start.15 = (bf16[192,768]{1,0:T(8,128)(2,1)S(1)}, bf16[192,768]{1,0:T(8,128)(2,1)S(1)}, u32[]{:S(2)}, u32[]{:S(2)}) collective-permute-start(bf16[192,768]{1,0:T(8,128)(2,1)S(1)} %get-tuple-element.210.refs_1_), channel_id=1, source_target_pairs={{0,16},{4,20},{8,24},{12,28},{16,0},{20,4},{24,8},{28,12},{1,17},{... | collective-permute-start | bytes 884744 | tf_op jit(solution)/shard_map/ppermute | solution.py:224
  76.7 10.0 %collective-permute-start.13 = (bf16[128,768]{1,0:T(8,128)(2,1)S(1)}, bf16[128,768]{1,0:T(8,128)(2,1)S(1)}, u32[]{:S(2)}, u32[]{:S(2)}) collective-permute-start(bf16[128,768]{1,0:T(8,128)(2,1)S(1)} %get-tuple-element.202), channel_id=1, source_target_pairs={{0,3},{1,0},{2,1},{3,2},{4,7},{5,4},{6,5},{7,6},{8,11},{9,8},{10,9... | collective-permute-start | bytes 589832 | tf_op jit(solution)/shard_map/ppermute | solution.py:1067
  79.6 17.3 %collective-permute-start.16 = (bf16[192,768]{1,0:T(8,128)(2,1)S(1)}, bf16[192,768]{1,0:T(8,128)(2,1)S(1)}, u32[]{:S(2)}, u32[]{:S(2)}) collective-permute-start(bf16[192,768]{1,0:T(8,128)(2,1)S(1)} %get-tuple-element.211.refs_2_), channel_id=1, source_target_pairs={{0,8},{4,12},{8,0},{12,4},{16,24},{20,28},{24,16},{28,20},{1,9},{5... | collective-permute-start | bytes 884744 | tf_op jit(solution)/shard_map/ppermute | solution.py:224
  85.0 11.9 %collective-permute-start.17 = (bf16[192,768]{1,0:T(8,128)(2,1)S(1)}, bf16[192,768]{1,0:T(8,128)(2,1)S(1)}, u32[]{:S(2)}, u32[]{:S(2)}) collective-permute-start(bf16[192,768]{1,0:T(8,128)(2,1)S(1)} %get-tuple-element.212.refs_3_), channel_id=1, source_target_pairs={{0,16},{4,20},{8,24},{12,28},{16,0},{20,4},{24,8},{28,12},{1,17},{... | collective-permute-start | bytes 884744 | tf_op jit(solution)/shard_map/ppermute | solution.py:224
  87.2 19.0 %collective-permute-start.18 = (bf16[128,768]{1,0:T(8,128)(2,1)S(1)}, bf16[128,768]{1,0:T(8,128)(2,1)S(1)}, u32[]{:S(2)}, u32[]{:S(2)}) collective-permute-start(bf16[128,768]{1,0:T(8,128)(2,1)S(1)} %get-tuple-element.216), channel_id=1, source_target_pairs={{0,2},{1,3},{2,0},{3,1},{4,6},{5,7},{6,4},{7,5},{8,10},{9,11},{10,... | collective-permute-start | bytes 589832 | tf_op jit(solution)/shard_map/ppermute | solution.py:1067
  93.1 13.0 %collective-permute-start.19 = (bf16[128,768]{1,0:T(8,128)(2,1)S(1)}, bf16[128,768]{1,0:T(8,128)(2,1)S(1)}, u32[]{:S(2)}, u32[]{:S(2)}) collective-permute-start(bf16[128,768]{1,0:T(8,128)(2,1)S(1)} %get-tuple-element.217), channel_id=1, source_target_pairs={{0,1},{1,2},{2,3},{3,0},{4,5},{5,6},{6,7},{7,4},{8,9},{9,10},{10,1... | collective-permute-start | bytes 589832 | tf_op jit(solution)/shard_map/ppermute | solution.py:1067
  96.4 10.4 %collective-permute-start.20 = (bf16[128,768]{1,0:T(8,128)(2,1)S(1)}, bf16[128,768]{1,0:T(8,128)(2,1)S(1)}, u32[]{:S(2)}, u32[]{:S(2)}) collective-permute-start(bf16[128,768]{1,0:T(8,128)(2,1)S(1)} %get-tuple-element.218), channel_id=1, source_target_pairs={{0,3},{1,0},{2,1},{3,2},{4,7},{5,4},{6,5},{7,6},{8,11},{9,8},{10,9... | collective-permute-start | bytes 589832 | tf_op jit(solution)/shard_map/ppermute | solution.py:1067
  97.2 18.6 %collective-permute-start.21 = (bf16[384,768]{1,0:T(8,128)(2,1)S(1)}, bf16[384,768]{1,0:T(8,128)(2,1)S(1)}, u32[]{:S(2)}, u32[]{:S(2)}) collective-permute-start(bf16[384,768]{1,0:T(8,128)(2,1)S(1)} %get-tuple-element.228.own_a), channel_id=1, source_target_pairs={{0,16},{4,20},{8,24},{12,28},{16,0},{20,4},{24,8},{28,12},{1,17},{... | collective-permute-start | bytes 1769480 | tf_op jit(solution)/shard_map/ppermute | solution.py:224
  97.8 18.1 %collective-permute-start.22 = (bf16[384,768]{1,0:T(8,128)(2,1)S(1)}, bf16[384,768]{1,0:T(8,128)(2,1)S(1)}, u32[]{:S(2)}, u32[]{:S(2)}) collective-permute-start(bf16[384,768]{1,0:T(8,128)(2,1)S(1)} %get-tuple-element.229.own_b), channel_id=1, source_target_pairs={{0,8},{4,12},{8,0},{12,4},{16,24},{20,28},{24,16},{28,20},{1,9},{5... | collective-permute-start | bytes 1769480 | tf_op jit(solution)/shard_map/ppermute | solution.py:224
  116.2 2.1 %collective-permute-start.23 = (bf16[400,768]{1,0:T(8,128)(2,1)S(1)}, bf16[400,768]{1,0:T(8,128)(2,1)S(1)}, u32[]{:S(2)}, u32[]{:S(2)}) collective-permute-start(bf16[400,768]{1,0:T(8,128)(2,1)S(1)} %get-tuple-element.230), channel_id=1, source_target_pairs={{0,4},{4,0},{8,12},{12,8},{16,20},{20,16},{24,28},{28,24},{1,5},{5... | collective-permute-start | bytes 1843208 | tf_op jit(solution)/shard_map/ppermute | solution.py:224
  116.3 13.8 %collective-permute-start.26 = (bf16[768,768]{1,0:T(8,128)(2,1)S(1)}, bf16[768,768]{1,0:T(8,128)(2,1)S(1)}, u32[]{:S(2)}, u32[]{:S(2)}) collective-permute-start(bf16[768,768]{1,0:T(8,128)(2,1)S(1)} %fold_feed_last.1.mine), channel_id=1, source_target_pairs={{0,4},{4,0},{8,12},{12,8},{16,20},{20,16},{24,28},{28,24},{1,5},{5... | collective-permute-start | bytes 3538952 | tf_op jit(solution)/shard_map/ppermute | solution.py:224
  118.4 9.8 %collective-permute-start.24 = (bf16[208,768]{1,0:T(8,128)(2,1)S(1)}, bf16[208,768]{1,0:T(8,128)(2,1)S(1)}, u32[]{:S(2)}, u32[]{:S(2)}) collective-permute-start(bf16[208,768]{1,0:T(8,128)(2,1)S(1)} %get-tuple-element.239.own_a), channel_id=1, source_target_pairs={{0,8},{4,12},{8,0},{12,4},{16,24},{20,28},{24,16},{28,20},{1,9},{5... | collective-permute-start | bytes 958472 | tf_op jit(solution)/shard_map/ppermute | solution.py:224
  119.5 8.8 %collective-permute-start.25 = (bf16[192,768]{1,0:T(8,128)(2,1)S(1)}, bf16[192,768]{1,0:T(8,128)(2,1)S(1)}, u32[]{:S(2)}, u32[]{:S(2)}) collective-permute-start(bf16[192,768]{1,0:T(8,128)(2,1)S(1)} %get-tuple-element.240.own_b), channel_id=1, source_target_pairs={{0,16},{4,20},{8,24},{12,28},{16,0},{20,4},{24,8},{28,12},{1,17},{... | collective-permute-start | bytes 884744 | tf_op jit(solution)/shard_map/ppermute | solution.py:224
  120.0 10.0 %copy-start.5 = (f32[2,768]{1,0:T(2,128)S(1)}, f32[2,768]{1,0:T(2,128)}, u32[]{:S(2)}) copy-start(f32[2,768]{1,0:T(2,128)} %wide_old.1) | copy-start | bytes 18436
  128.3 11.0 %copy-start.2 = (f32[4,2,768]{2,1,0:T(2,128)S(1)}, f32[4,2,768]{2,1,0:T(2,128)}, u32[]{:S(2)}) copy-start(f32[4,2,768]{2,1,0:T(2,128)} %stats.3) | copy-start | bytes 73732
  128.4 8.6 %collective-permute-start.27 = (bf16[208,768]{1,0:T(8,128)(2,1)S(1)}, bf16[208,768]{1,0:T(8,128)(2,1)S(1)}, u32[]{:S(2)}, u32[]{:S(2)}) collective-permute-start(bf16[208,768]{1,0:T(8,128)(2,1)S(1)} %get-tuple-element.246.own_a), channel_id=1, source_target_pairs={{0,16},{4,20},{8,24},{12,28},{16,0},{20,4},{24,8},{28,12},{1,17},{... | collective-permute-start | bytes 958472 | tf_op jit(solution)/shard_map/ppermute | solution.py:224
  129.0 7.7 %collective-permute-start.28 = (bf16[192,768]{1,0:T(8,128)(2,1)S(1)}, bf16[192,768]{1,0:T(8,128)(2,1)S(1)}, u32[]{:S(2)}, u32[]{:S(2)}) collective-permute-start(bf16[192,768]{1,0:T(8,128)(2,1)S(1)} %get-tuple-element.247.own_b), channel_id=1, source_target_pairs={{0,8},{4,12},{8,0},{12,4},{16,24},{20,28},{24,16},{28,20},{1,9},{5... | collective-permute-start | bytes 884744 | tf_op jit(solution)/shard_map/ppermute | solution.py:224
  137.0 13.5 %copy-start.3 = (f32[4,768]{1,0:T(4,128)S(1)}, f32[4,768]{1,0:T(4,128)}, u32[]{:S(2)}) copy-start(f32[4,768]{1,0:T(4,128)} %vec_moment.1) | copy-start | bytes 36868
  137.0 13.5 %copy-start.4 = (f32[2,768]{1,0:T(2,128)S(1)}, f32[2,768]{1,0:T(2,128)}, u32[]{:S(2)}) copy-start(f32[2,768]{1,0:T(2,128)} %narrow_old.1) | copy-start | bytes 18436
  137.2 2.1 %collective-permute-start.29 = (bf16[384,768]{1,0:T(8,128)(2,1)S(1)}, bf16[384,768]{1,0:T(8,128)(2,1)S(1)}, u32[]{:S(2)}, u32[]{:S(2)}) collective-permute-start(bf16[384,768]{1,0:T(8,128)(2,1)S(1)} %get-tuple-element.249.even), channel_id=1, source_target_pairs={{0,4},{4,0},{8,12},{12,8},{16,20},{20,16},{24,28},{28,24},{1,5},{5... | collective-permute-start | bytes 1769480 | tf_op jit(solution)/shard_map/ppermute | solution.py:224
  140.9 7.6 %collective-permute-start.32 = (bf16[32,768]{1,0:T(8,128)(2,1)S(1)}, bf16[32,768]{1,0:T(8,128)(2,1)S(1)}, u32[]{:S(2)}, u32[]{:S(2)}) collective-permute-start(bf16[32,768]{1,0:T(8,128)(2,1)S(1)} %get-tuple-element.263.share), channel_id=1, source_target_pairs={{0,3},{1,2},{2,1},{3,0},{4,7},{5,6},{6,5},{7,4},{8,11},{9,10},{10,... | collective-permute-start | bytes 147464 | tf_op jit(solution)/shard_map/ppermute | solution.py:1067
  144.7 5.0 %collective-permute-start.31 = (bf16[32,768]{1,0:T(8,128)(2,1)S(1)}, bf16[32,768]{1,0:T(8,128)(2,1)S(1)}, u32[]{:S(2)}, u32[]{:S(2)}) collective-permute-start(bf16[32,768]{1,0:T(8,128)(2,1)S(1)} %get-tuple-element.263.share), channel_id=1, source_target_pairs={{0,2},{1,3},{2,0},{3,1},{4,6},{5,7},{6,4},{7,5},{8,10},{9,11},{10,... | collective-permute-start | bytes 147464 | tf_op jit(solution)/shard_map/ppermute | solution.py:1067
  146.4 4.1 %collective-permute-start.30 = (bf16[32,768]{1,0:T(8,128)(2,1)S(1)}, bf16[32,768]{1,0:T(8,128)(2,1)S(1)}, u32[]{:S(2)}, u32[]{:S(2)}) collective-permute-start(bf16[32,768]{1,0:T(8,128)(2,1)S(1)} %get-tuple-element.263.share), channel_id=1, source_target_pairs={{0,1},{1,0},{2,3},{3,2},{4,5},{5,4},{6,7},{7,6},{8,9},{9,8},{10,11... | collective-permute-start | bytes 147464 | tf_op jit(solution)/shard_map/ppermute | solution.py:1067

commit v2 on v1

--- a/solution.py
+++ b/solution.py
@@ -68,7 +68,7 @@
 STAGED = 8
 VEC_ROWS = 16
 TOKEN_STEPS = (0, -2, -1, -3)
-BRANCH_STEPS = (0, 1, 2, 3)
+BRANCH_STEPS = (0, 2, 1, 3)
 BACK_STEPS = (0, 2, 1, 3)
 FIRST_STEPS = (0, 1, 2, 3)
 MIX_STEPS = (0, 2, 1, 3)
@@ -1143,10 +1143,10 @@
     *d_mix, vec_part, attn_keep, attn_send = mix_second(first, attn_low, feats, x_slice, mixed_slice, sums)
     if staged:
         feed_even = fold_feed_last(feed_a, got_a, feed_b, got_b)
-        attn_send, feed_even = lax.optimization_barrier((attn_send, feed_even))
         received = across(attn_send, 1)
+        attn_keep, feed_even = lax.optimization_barrier((attn_keep, feed_even))
+        vec_part, attn_a, attn_b = fold_first(attn_keep, received, vec_part)
         feed_odd = across(feed_even, 1)
-        vec_part, attn_a, attn_b = fold_first(attn_keep, received, vec_part)
         got_a, got_b = across(attn_a, 2), across(attn_b, 4)
     else:
         feed_even, feed_odd, attn_even, attn_odd, vec_part = lax.psum(

time: 156 us -> 155 us (level)
  starting transfers between devices: 58.4 us -> 54.8 us
  waiting for transfers between devices: 42.3 us -> 45 us
    ppermute x18, waiting for transfers between devices: 31.9 us -> 35.7 us  [exchange(): lax.ppermute(part, 'mp', [(i, target(i, step, ranks)) for i in range(rank...]
    ppermute x18, starting transfers between devices: 45.7 us -> 43 us  [exchange(): lax.ppermute(part, 'mp', [(i, target(i, step, ranks)) for i in range(rank...]
  transfers between devices with their start and end apart: 33 -> 33, of which waited for: 15 -> 14; matrix products, arithmetic and copies ran while one was open for 0% -> 0% of each run, Pallas kernels for 22% -> 22%
where the time goes in v2:
time: 155 us
  starting transfers between devices  54.8 us (35%)
  Pallas kernels  53.2 us (34%)
  waiting for transfers between devices  45 us (29%)
    ppermute x18, starting transfers between devices, exchange(): lax.ppermute(part, 'mp', [(i, target(i, step, ranks)) for i in range(rank...  43 us
    ppermute x18, waiting for transfers between devices, exchange(): lax.ppermute(part, 'mp', [(i, target(i, step, ranks)) for i in range(rank...  35.7 us
    ppermute x15, starting transfers between devices, across(): return lax.ppermute(block, 'dp', [(i, i ^ bit) for i in range(STAGED)])  11.8 us
    ppermute x15, waiting for transfers between devices, across(): return lax.ppermute(block, 'dp', [(i, i ^ bit) for i in range(STAGED)])  9.38 us
    pallas_call x1, Pallas kernels, prepare(): pl.pallas_call(functools.partial(prepare_kernel, seqs, tokens_pack), grid...  8.83 us
    pallas_call x1, Pallas kernels, forward(): pl.pallas_call(functools.partial(forward_kernel, local), out_shape=[near(...  8.15 us
    pallas_call x1, Pallas kernels, update(): pl.pallas_call(functools.partial(update_kernel, hidden_all), in_specs=[pl...  4.96 us
    pallas_call x1, Pallas kernels, mix_second(): pl.pallas_call(mix_second_kernel, out_shape=[near((tokens, width), bf16)]...  4.65 us
  transfers between devices with their start and end apart: 33, of which 14 were waited for; matrix products, arithmetic and copies ran while one was open for 0% of the time, Pallas kernels for 22%

profile of v2, /device:TPU:0, one launch (start us, length us, event | category | flops | bytes accessed | tf_op | source)
XLA Modules:
  0.0 154.8 jit_solution(15658813534877121725)
XLA Ops:
  0.7 3.1 %collective-permute-start.1 = (bf16[128,768]{1,0:T(8,128)(2,1)}, bf16[128,768]{1,0:T(8,128)(2,1)S(1)}, u32[]{:S(2)}, u32[]{:S(2)}) collective-permute-start(bf16[128,768]{1,0:T(8,128)(2,1)} %x0.1), channel_id=1, source_target_pairs={{0,1},{1,0},{2,3},{3,2},{4,5},{5,4},{6,7},{7,6},{8,9},{9,8},{10,11... | collective-permute-start | bytes 589832 | tf_op jit(solution)/shard_map/ppermute | solution.py:1067
  3.8 2.6 %collective-permute-start = (bf16[128,768]{1,0:T(8,128)(2,1)}, bf16[128,768]{1,0:T(8,128)(2,1)S(1)}, u32[]{:S(2)}, u32[]{:S(2)}) collective-permute-start(bf16[128,768]{1,0:T(8,128)(2,1)} %x0.1), channel_id=1, source_target_pairs={{0,2},{1,3},{2,0},{3,1},{4,6},{5,7},{6,4},{7,5},{8,10},{9,11},{10,... | collective-permute-start | bytes 589832 | tf_op jit(solution)/shard_map/ppermute | solution.py:1067
  6.3 0.7 copy-done.6
  7.0 8.8 %prepare.1 = (bf16[4,768,768]{2,1,0:T(8,128)(2,1)S(1)}, bf16[768,768]{1,0:T(8,128)(2,1)S(1)}, bf16[768,768]{1,0:T(8,128)(2,1)S(1)}, f32[512,512]{1,0:T(8,128)S(1...) custom-call(s32[1,8]{1,0:T(1,128)S(1)} %copy-done.6, f32[4,768,768]{2,1,0:T(8,128)} %attn_weight.1, ...), custom_call_target="tpu_custom_call" | custom-call | flops 10000000 | bytes 22000000 | tf_op jit(solution)/shard_map/prepare/pallas_call | solution.py:275
  15.9 5.3 %collective-permute-done.x1 = bf16[128,768]{1,0:T(8,128)(2,1)S(1)} collective-permute-done((bf16[128,768]{1,0:T(8,128)(2,1)}, bf16[128,768]{1,0:T(8,128)(2,1)S(1)}, u32[]{:S(2)}, u32[]{:S(2)}) %collective-permute-start) | collective-permute-done | bytes 196640 | tf_op jit(solution)/shard_map/ppermute | solution.py:1067
  21.1 8.1 %forward.1 = (bf16[512,768]{1,0:T(8,128)(2,1)S(1)}, bf16[512,768]{1,0:T(8,128)(2,1)S(1)}, bf16[512,768]{1,0:T(8,128)(2,1)S(1)}, bf16[512,768]{1,0:T(8,128)(2,1)S...) custom-call(bf16[128,768]{1,0:T(8,128)(2,1)S(1)} %copy-done.7, ...), custom_call_target="tpu_custom_call" | custom-call | flops 8000000000 | bytes 20000000 | tf_op jit(solution)/shard_map/forward/pallas_call | solution.py:424
  29.3 4.4 %collective-permute-start.3 = (bf16[128,768]{1,0:T(8,128)(2,1)S(1)}, bf16[128,768]{1,0:T(8,128)(2,1)S(1)}, u32[]{:S(2)}, u32[]{:S(2)}) collective-permute-start(bf16[128,768]{1,0:T(8,128)(2,1)S(1)} %get-tuple-element.154), channel_id=1, source_target_pairs={{0,2},{1,3},{2,0},{3,1},{4,6},{5,7},{6,4},{7,5},{8,10},{9,11},{10,... | collective-permute-start | bytes 589832 | tf_op jit(solution)/shard_map/ppermute | solution.py:1067
  33.7 3.8 %collective-permute-start.5 = (bf16[128,768]{1,0:T(8,128)(2,1)S(1)}, bf16[128,768]{1,0:T(8,128)(2,1)S(1)}, u32[]{:S(2)}, u32[]{:S(2)}) collective-permute-start(bf16[128,768]{1,0:T(8,128)(2,1)S(1)} %get-tuple-element.156), channel_id=1, source_target_pairs={{0,3},{1,0},{2,1},{3,2},{4,7},{5,4},{6,5},{7,6},{8,11},{9,8},{10,9... | collective-permute-start | bytes 589832 | tf_op jit(solution)/shard_map/ppermute | solution.py:1067
  37.5 4.3 %slopes.1 = (bf16[6144,512]{1,0:T(8,128)(2,1)S(1)}, bf16[512,768]{1,0:T(8,128)(2,1)S(1)}, bf16[512,768]{1,0:T(8,128)(2,1)S(1)}, f32[512,768]{1,0:T(8,128)S(1)}) custom-call(bf16[512,768]{1,0:T(8,128)(2,1)S(1)} %get-tuple-element.158.query_feat.refs_10_.refs_11_, bf16[512,768]{1,0:T(8,128)(2,1)S(1)} %get-tuple-element.159.key_feat.refs_11_.refs_12_, ...), custom_call_target="tpu_custom_call" | custom-call | tf_op jit(solution)/shard_map/slopes/pallas_call | solution.py:466
  41.8 5.3 %collective-permute-done.3.refs_1_ = bf16[128,768]{1,0:T(8,128)(2,1)S(1)} collective-permute-done((bf16[128,768]{1,0:T(8,128)(2,1)S(1)}, bf16[128,768]{1,0:T(8,128)(2,1)S(1)}, u32[]{:S(2)}, u32[]{:S(2)}) %collective-permute-start.3) | collective-permute-done | bytes 196640 | tf_op jit(solution)/shard_map/ppermute | solution.py:1067
  47.2 0.4 middle.1
  47.6 3.5 %collective-permute-start.6 = (bf16[128,768]{1,0:T(8,128)(2,1)S(1)}, bf16[128,768]{1,0:T(8,128)(2,1)S(1)}, u32[]{:S(2)}, u32[]{:S(2)}) collective-permute-start(bf16[128,768]{1,0:T(8,128)(2,1)S(1)} %get-tuple-element.179), channel_id=1, source_target_pairs={{0,2},{1,3},{2,0},{3,1},{4,6},{5,7},{6,4},{7,5},{8,10},{9,11},{10,... | collective-permute-start | bytes 589832 | tf_op jit(solution)/shard_map/ppermute | solution.py:1067
  51.1 0.3 collective-permute-start.7
  51.4 3.5 %collective-permute-start.8 = (bf16[128,768]{1,0:T(8,128)(2,1)S(1)}, bf16[128,768]{1,0:T(8,128)(2,1)S(1)}, u32[]{:S(2)}, u32[]{:S(2)}) collective-permute-start(bf16[128,768]{1,0:T(8,128)(2,1)S(1)} %get-tuple-element.181), channel_id=1, source_target_pairs={{0,3},{1,0},{2,1},{3,2},{4,7},{5,4},{6,5},{7,6},{8,11},{9,8},{10,9... | collective-permute-start | bytes 589832 | tf_op jit(solution)/shard_map/ppermute | solution.py:1067
  54.9 1.2 own_columns.1
  56.1 8.8 %collective-permute-done.6.refs_1_ = bf16[128,768]{1,0:T(8,128)(2,1)S(1)} collective-permute-done((bf16[128,768]{1,0:T(8,128)(2,1)S(1)}, bf16[128,768]{1,0:T(8,128)(2,1)S(1)}, u32[]{:S(2)}, u32[]{:S(2)}) %collective-permute-start.6) | collective-permute-done | bytes 196640 | tf_op jit(solution)/shard_map/ppermute | solution.py:1067
  64.9 1.7 %feed_back.1 = (bf16[512,768]{1,0:T(8,128)(2,1)S(1)}, bf16[512,768]{1,0:T(8,128)(2,1)S(1)}, f32[128,768]{1,0:T(8,128)S(1)}, bf16[128,768]{1,0:T(8,128)(2,1)S(1)}...) custom-call(bf16[128,768]{1,0:T(8,128)(2,1)S(1)} %get-tuple-element.178.refs_0_, ...), custom_call_target="tpu_custom_call" | custom-call | flops 1200000000 | bytes 9000000 | tf_op jit(solution)/shard_map/feed_back/pallas_call | solution.py:524
  66.6 1.4 feed_grads.1
  68.1 0.5 collective-permute-start.10
  68.6 3.0 %collective-permute-start.11 = (bf16[128,768]{1,0:T(8,128)(2,1)S(1)}, bf16[128,768]{1,0:T(8,128)(2,1)S(1)}, u32[]{:S(2)}, u32[]{:S(2)}) collective-permute-start(bf16[128,768]{1,0:T(8,128)(2,1)S(1)} %get-tuple-element.200), channel_id=1, source_target_pairs={{0,1},{1,2},{2,3},{3,0},{4,5},{5,6},{6,7},{7,4},{8,9},{9,10},{10,1... | collective-permute-start | bytes 589832 | tf_op jit(solution)/shard_map/ppermute | solution.py:1067
  71.6 1.3 collective-permute-start.12
  73.0 0.1 fold_first.4
  73.1 1.5 collective-permute-start.14
  74.6 1.5 collective-permute-start.15
  76.2 2.9 %collective-permute-start.13 = (bf16[128,768]{1,0:T(8,128)(2,1)S(1)}, bf16[128,768]{1,0:T(8,128)(2,1)S(1)}, u32[]{:S(2)}, u32[]{:S(2)}) collective-permute-start(bf16[128,768]{1,0:T(8,128)(2,1)S(1)} %get-tuple-element.202), channel_id=1, source_target_pairs={{0,3},{1,0},{2,1},{3,2},{4,7},{5,4},{6,5},{7,6},{8,11},{9,8},{10,9... | collective-permute-start | bytes 589832 | tf_op jit(solution)/shard_map/ppermute | solution.py:1067
  79.1 0.6 collective-permute-start.16
  79.8 6.1 %collective-permute-done.12.refs_2_ = bf16[128,768]{1,0:T(8,128)(2,1)S(1)} collective-permute-done((bf16[128,768]{1,0:T(8,128)(2,1)S(1)}, bf16[128,768]{1,0:T(8,128)(2,1)S(1)}, u32[]{:S(2)}, u32[]{:S(2)}) %collective-permute-start.12) | collective-permute-done | bytes 196640 | tf_op jit(solution)/shard_map/ppermute | solution.py:1067
  85.9 1.5 collective-permute-start.17
  87.4 0.4 first_back.1
  87.8 4.8 %collective-permute-start.18 = (bf16[128,768]{1,0:T(8,128)(2,1)S(1)}, bf16[128,768]{1,0:T(8,128)(2,1)S(1)}, u32[]{:S(2)}, u32[]{:S(2)}) collective-permute-start(bf16[128,768]{1,0:T(8,128)(2,1)S(1)} %get-tuple-element.216), channel_id=1, source_target_pairs={{0,2},{1,3},{2,0},{3,1},{4,6},{5,7},{6,4},{7,5},{8,10},{9,11},{10,... | collective-permute-start | bytes 589832 | tf_op jit(solution)/shard_map/ppermute | solution.py:1067
  92.6 3.3 %collective-permute-start.19 = (bf16[128,768]{1,0:T(8,128)(2,1)S(1)}, bf16[128,768]{1,0:T(8,128)(2,1)S(1)}, u32[]{:S(2)}, u32[]{:S(2)}) collective-permute-start(bf16[128,768]{1,0:T(8,128)(2,1)S(1)} %get-tuple-element.217), channel_id=1, source_target_pairs={{0,1},{1,2},{2,3},{3,0},{4,5},{5,6},{6,7},{7,4},{8,9},{9,10},{10,1... | collective-permute-start | bytes 589832 | tf_op jit(solution)/shard_map/ppermute | solution.py:1067
  95.9 0.5 collective-permute-start.20
  96.4 0.3 fold_feed.1
  96.7 0.6 collective-permute-start.21
  97.3 1.0 collective-permute-start.22
  98.2 7.4 %collective-permute-done.18.a1 = bf16[128,768]{1,0:T(8,128)(2,1)S(1)} collective-permute-done((bf16[128,768]{1,0:T(8,128)(2,1)S(1)}, bf16[128,768]{1,0:T(8,128)(2,1)S(1)}, u32[]{:S(2)}, u32[]{:S(2)}) %collective-permute-start.18) | collective-permute-done | bytes 196640 | tf_op jit(solution)/shard_map/ppermute | solution.py:1067
  105.6 0.7 collective-permute-done.20.a3
  106.3 4.3 %mix_first.1 = (bf16[512,768]{1,0:T(8,128)(2,1)S(1)}, bf16[512,768]{1,0:T(8,128)(2,1)S(1)}, bf16[512,768]{1,0:T(8,128)(2,1)S(1)}, bf16[512,384]{1,0:T(8,128)(2,1...) custom-call(bf16[128,768]{1,0:T(8,128)(2,1)S(1)} %get-tuple-element.215.a0, ...), custom_call_target="tpu_custom_call" | custom-call | flops 6000000000 | bytes 18000000 | tf_op jit(solution)/shard_map/mix_first/pallas_call | solution.py:691
  110.6 4.7 %mix_second.1 = (bf16[512,768]{1,0:T(8,128)(2,1)S(1)}, bf16[512,768]{1,0:T(8,128)(2,1)S(1)}, bf16[512,768]{1,0:T(8,128)(2,1)S(1)}, f32[8,768]{1,0:T(8,128)S(1)},...) custom-call(bf16[512,768]{1,0:T(8,128)(2,1)S(1)} %get-tuple-element.219.d_attn, ...), custom_call_target="tpu_custom_call" | custom-call | flops 6000000000 | bytes 18000000 | tf_op jit(solution)/shard_map/mix_second/pallas_call | solution.py:749
  115.4 0.3 fold_feed_last.1.mine
  115.7 0.5 collective-permute-start.26
  116.2 1.2 collective-permute-done.23.received
  117.4 0.1 fold_first.5
  117.5 0.6 collective-permute-start.24
  118.2 1.3 collective-permute-start.25
  119.4 4.6 %tokens_back.1 = (f32[128,768]{1,0:T(8,128)}, f32[4,192,768]{2,1,0:T(8,128)S(1)}, f32[768,768]{1,0:T(8,128)S(1)}, f32[768,768]{1,0:T(8,128)S(1)}) custom-call(bf16[512,768]{1,0:T(8,128)(2,1)S(1)} %get-tuple-element.233.d_query, bf16[512,768]{1,0:T(8,128)(2,1)S(1)} %get-tuple-element.234.d_key, bf16[512,768]{1,0:T(8,128)(2,1)S(1)} %get-tuple-element.235.d_value, ...), custom_call_target="tpu_custom_call" | custom-call | tf_op jit(solution)/shard_map/tokens_back/pallas_call | solution.py:790
  124.0 2.9 %collective-permute-done.25.got_b = bf16[192,768]{1,0:T(8,128)(2,1)S(1)} collective-permute-done((bf16[192,768]{1,0:T(8,128)(2,1)S(1)}, bf16[192,768]{1,0:T(8,128)(2,1)S(1)}, u32[]{:S(2)}, u32[]{:S(2)}) %collective-permute-start.25) | collective-permute-done | bytes 294944 | tf_op jit(solution)/shard_map/ppermute | solution.py:224
  126.9 0.3 collective-permute-done.24.got_a
  127.2 0.2 fold_second.1
  127.4 1.1 collective-permute-start.27
  128.4 0.8 collective-permute-start.28
  129.3 3.9 %feed_stats.1 = (f32[768,768]{1,0:T(8,128)}, f32[768,768]{1,0:T(8,128)}, f32[2,768]{1,0:T(2,128)}, f32[1536,768]{1,0:T(8,128)S(1)}, f32[2,768]{1,0:T(2,128)S(1)}, /*index=5*/f32[8,768]{1,0:T(8,128)S(1)}) custom-call(bf16[768,768]{1,0:T(8,128)(2,1)S(1)} %fold_feed_last.1.mine, bf16[768,768]{1,0:T(8,128)(2,1)S(1)} %collective-permute-done.26.other, ...), custom_call_target="tpu_custom_call" | custom-call | tf_op jit(solution)/shard_map/feed_stats/pallas_call | solution.py:916
  133.2 2.9 %collective-permute-done.28.got_b = bf16[192,768]{1,0:T(8,128)(2,1)S(1)} collective-permute-done((bf16[192,768]{1,0:T(8,128)(2,1)S(1)}, bf16[192,768]{1,0:T(8,128)(2,1)S(1)}, u32[]{:S(2)}, u32[]{:S(2)}) %collective-permute-start.28) | collective-permute-done | bytes 294944 | tf_op jit(solution)/shard_map/ppermute | solution.py:224
  136.1 0.1 collective-permute-done.27.got_a
  136.2 0.1 fold_last.1
  136.4 2.0 %collective-permute-done.29.odd = bf16[384,768]{1,0:T(8,128)(2,1)S(1)} collective-permute-done((bf16[384,768]{1,0:T(8,128)(2,1)S(1)}, bf16[384,768]{1,0:T(8,128)(2,1)S(1)}, u32[]{:S(2)}, u32[]{:S(2)}) %collective-permute-start.29) | collective-permute-done | bytes 589856 | tf_op jit(solution)/shard_map/ppermute | solution.py:224
  138.4 1.7 %attn_stats.1 = (f32[768,768]{1,0:T(8,128)S(1)}, f32[4,192]{1,0:T(4,128)S(1)}, bf16[32,768]{1,0:T(8,128)(2,1)S(1)}) custom-call(bf16[384,768]{1,0:T(8,128)(2,1)S(1)} %get-tuple-element.249.even, bf16[384,768]{1,0:T(8,128)(2,1)S(1)} %collective-permute-done.29.odd, f32[8,768]{1,0:T(8,128)S(1)} %get-tuple-element.250.vec, f32[4,2,768]{2,1,0:T(2,128)S(1)} %copy-done.2, ...), custom_call_target="tpu_custom_call" | custom-call | tf_op jit(solution)/shard_map/attn_stats/pallas_call | solution.py:858
  140.1 3.7 %collective-permute-start.32 = (bf16[32,768]{1,0:T(8,128)(2,1)S(1)}, bf16[32,768]{1,0:T(8,128)(2,1)S(1)}, u32[]{:S(2)}, u32[]{:S(2)}) collective-permute-start(bf16[32,768]{1,0:T(8,128)(2,1)S(1)} %get-tuple-element.263.share), channel_id=1, source_target_pairs={{0,3},{1,2},{2,1},{3,0},{4,7},{5,6},{6,5},{7,4},{8,11},{9,10},{10,... | collective-permute-start | bytes 147464 | tf_op jit(solution)/shard_map/ppermute | solution.py:1067
  143.8 1.8 %collective-permute-start.31 = (bf16[32,768]{1,0:T(8,128)(2,1)S(1)}, bf16[32,768]{1,0:T(8,128)(2,1)S(1)}, u32[]{:S(2)}, u32[]{:S(2)}) collective-permute-start(bf16[32,768]{1,0:T(8,128)(2,1)S(1)} %get-tuple-element.263.share), channel_id=1, source_target_pairs={{0,2},{1,3},{2,0},{3,1},{4,6},{5,7},{6,4},{7,5},{8,10},{9,11},{10,... | collective-permute-start | bytes 147464 | tf_op jit(solution)/shard_map/ppermute | solution.py:1067
  145.6 0.5 collective-permute-start.30
  146.1 1.6 %attn_out.1 = (f32[4,192,768]{2,1,0:T(8,128)}, f32[4,192]{1,0:T(4,128)}) custom-call(f32[768,768]{1,0:T(8,128)S(1)} %get-tuple-element.257.total.attn_grad, f32[4,192]{1,0:T(4,128)S(1)} %get-tuple-element.253.rows.attn_rows), custom_call_target="tpu_custom_call" | custom-call | tf_op jit(solution)/shard_map/attn_out/pallas_call | solution.py:876
  147.6 1.2 collective-permute-done.31.share2
  148.8 0.8 collective-permute-done.30.share1
  149.7 5.0 %update.1 = (f32[4,192,768]{2,1,0:T(8,128)}, bf16[4,192,768]{2,1,0:T(8,128)(2,1)}, f32[768,768]{1,0:T(8,128)}, bf16[768,768]{1,0:T(8,128)(2,1)}, f32[768,768]{1,...) custom-call(f32[768,768]{1,0:T(8,128)S(1)} %get-tuple-element.257.to, ...), custom_call_target="tpu_custom_call" | custom-call | tf_op jit(solution)/shard_map/update/pallas_call | solution.py:1048
  (40 shorter events, 0.4 us)
Async XLA Ops:
  0.7 20.5 %copy-start.1 = (f32[4,768]{1,0:T(4,128)S(1)}, f32[4,768]{1,0:T(4,128)}, u32[]{:S(2)}) copy-start(f32[4,768]{1,0:T(4,128)} %vec.3) | copy-start | bytes 36868
  0.7 15.2 %collective-permute-start.1 = (bf16[128,768]{1,0:T(8,128)(2,1)}, bf16[128,768]{1,0:T(8,128)(2,1)S(1)}, u32[]{:S(2)}, u32[]{:S(2)}) collective-permute-start(bf16[128,768]{1,0:T(8,128)(2,1)} %x0.1), channel_id=1, source_target_pairs={{0,1},{1,0},{2,3},{3,2},{4,5},{5,4},{6,7},{7,6},{8,9},{9,8},{10,11... | collective-permute-start | bytes 589832 | tf_op jit(solution)/shard_map/ppermute | solution.py:1067
  3.8 17.4 %collective-permute-start = (bf16[128,768]{1,0:T(8,128)(2,1)}, bf16[128,768]{1,0:T(8,128)(2,1)S(1)}, u32[]{:S(2)}, u32[]{:S(2)}) collective-permute-start(bf16[128,768]{1,0:T(8,128)(2,1)} %x0.1), channel_id=1, source_target_pairs={{0,2},{1,3},{2,0},{3,1},{4,6},{5,7},{6,4},{7,5},{8,10},{9,11},{10,... | collective-permute-start | bytes 589832 | tf_op jit(solution)/shard_map/ppermute | solution.py:1067
  6.3 14.8 %collective-permute-start.2 = (bf16[128,768]{1,0:T(8,128)(2,1)}, bf16[128,768]{1,0:T(8,128)(2,1)S(1)}, u32[]{:S(2)}, u32[]{:S(2)}) collective-permute-start(bf16[128,768]{1,0:T(8,128)(2,1)} %x0.1), channel_id=1, source_target_pairs={{0,3},{1,2},{2,1},{3,0},{4,7},{5,6},{6,5},{7,4},{8,11},{9,10},{10,... | collective-permute-start | bytes 589832 | tf_op jit(solution)/shard_map/ppermute | solution.py:1067
  6.3 0.7 copy-start.6
  7.0 14.1 %copy-start.7 = (bf16[128,768]{1,0:T(8,128)(2,1)S(1)}, bf16[128,768]{1,0:T(8,128)(2,1)}, u32[]{:S(2)}) copy-start(bf16[128,768]{1,0:T(8,128)(2,1)} %x0.1) | copy-start | bytes 589828
  29.3 17.9 %copy-start = (bf16[128,768]{1,0:T(8,128)(2,1)S(1)}, bf16[128,768]{1,0:T(8,128)(2,1)}, u32[]{:S(2)}) copy-start(bf16[128,768]{1,0:T(8,128)(2,1)} %refs_5_.1) | copy-start | bytes 589828
  29.3 17.9 %collective-permute-start.3 = (bf16[128,768]{1,0:T(8,128)(2,1)S(1)}, bf16[128,768]{1,0:T(8,128)(2,1)S(1)}, u32[]{:S(2)}, u32[]{:S(2)}) collective-permute-start(bf16[128,768]{1,0:T(8,128)(2,1)S(1)} %get-tuple-element.154), channel_id=1, source_target_pairs={{0,2},{1,3},{2,0},{3,1},{4,6},{5,7},{6,4},{7,5},{8,10},{9,11},{10,... | collective-permute-start | bytes 589832 | tf_op jit(solution)/shard_map/ppermute | solution.py:1067
  33.7 13.5 %collective-permute-start.4 = (bf16[128,768]{1,0:T(8,128)(2,1)S(1)}, bf16[128,768]{1,0:T(8,128)(2,1)S(1)}, u32[]{:S(2)}, u32[]{:S(2)}) collective-permute-start(bf16[128,768]{1,0:T(8,128)(2,1)S(1)} %get-tuple-element.155), channel_id=1, source_target_pairs={{0,1},{1,2},{2,3},{3,0},{4,5},{5,6},{6,7},{7,4},{8,9},{9,10},{10,1... | collective-permute-start | bytes 589832 | tf_op jit(solution)/shard_map/ppermute | solution.py:1067
  33.7 13.5 %collective-permute-start.5 = (bf16[128,768]{1,0:T(8,128)(2,1)S(1)}, bf16[128,768]{1,0:T(8,128)(2,1)S(1)}, u32[]{:S(2)}, u32[]{:S(2)}) collective-permute-start(bf16[128,768]{1,0:T(8,128)(2,1)S(1)} %get-tuple-element.156), channel_id=1, source_target_pairs={{0,3},{1,0},{2,1},{3,2},{4,7},{5,4},{6,5},{7,6},{8,11},{9,8},{10,9... | collective-permute-start | bytes 589832 | tf_op jit(solution)/shard_map/ppermute | solution.py:1067
  47.6 17.3 %collective-permute-start.6 = (bf16[128,768]{1,0:T(8,128)(2,1)S(1)}, bf16[128,768]{1,0:T(8,128)(2,1)S(1)}, u32[]{:S(2)}, u32[]{:S(2)}) collective-permute-start(bf16[128,768]{1,0:T(8,128)(2,1)S(1)} %get-tuple-element.179), channel_id=1, source_target_pairs={{0,2},{1,3},{2,0},{3,1},{4,6},{5,7},{6,4},{7,5},{8,10},{9,11},{10,... | collective-permute-start | bytes 589832 | tf_op jit(solution)/shard_map/ppermute | solution.py:1067
  51.1 13.8 %collective-permute-start.7 = (bf16[128,768]{1,0:T(8,128)(2,1)S(1)}, bf16[128,768]{1,0:T(8,128)(2,1)S(1)}, u32[]{:S(2)}, u32[]{:S(2)}) collective-permute-start(bf16[128,768]{1,0:T(8,128)(2,1)S(1)} %get-tuple-element.180), channel_id=1, source_target_pairs={{0,1},{1,2},{2,3},{3,0},{4,5},{5,6},{6,7},{7,4},{8,9},{9,10},{10,1... | collective-permute-start | bytes 589832 | tf_op jit(solution)/shard_map/ppermute | solution.py:1067
  51.4 13.5 %collective-permute-start.8 = (bf16[128,768]{1,0:T(8,128)(2,1)S(1)}, bf16[128,768]{1,0:T(8,128)(2,1)S(1)}, u32[]{:S(2)}, u32[]{:S(2)}) collective-permute-start(bf16[128,768]{1,0:T(8,128)(2,1)S(1)} %get-tuple-element.181), channel_id=1, source_target_pairs={{0,3},{1,0},{2,1},{3,2},{4,7},{5,4},{6,5},{7,6},{8,11},{9,8},{10,9... | collective-permute-start | bytes 589832 | tf_op jit(solution)/shard_map/ppermute | solution.py:1067
  68.0 4.8 %collective-permute-start.9 = (bf16[384,768]{1,0:T(8,128)(2,1)S(1)}, bf16[384,768]{1,0:T(8,128)(2,1)S(1)}, u32[]{:S(2)}, u32[]{:S(2)}) collective-permute-start(bf16[384,768]{1,0:T(8,128)(2,1)S(1)} %get-tuple-element.192), channel_id=1, source_target_pairs={{0,4},{4,0},{8,12},{12,8},{16,20},{20,16},{24,28},{28,24},{1,5},{5... | collective-permute-start | bytes 1769480 | tf_op jit(solution)/shard_map/ppermute | solution.py:224
  68.1 4.9 %collective-permute-start.10 = (bf16[384,768]{1,0:T(8,128)(2,1)S(1)}, bf16[384,768]{1,0:T(8,128)(2,1)S(1)}, u32[]{:S(2)}, u32[]{:S(2)}) collective-permute-start(bf16[384,768]{1,0:T(8,128)(2,1)S(1)} %get-tuple-element.196), channel_id=1, source_target_pairs={{0,4},{4,0},{8,12},{12,8},{16,20},{20,16},{24,28},{28,24},{1,5},{5... | collective-permute-start | bytes 1769480 | tf_op jit(solution)/shard_map/ppermute | solution.py:224
  68.6 10.5 %collective-permute-start.11 = (bf16[128,768]{1,0:T(8,128)(2,1)S(1)}, bf16[128,768]{1,0:T(8,128)(2,1)S(1)}, u32[]{:S(2)}, u32[]{:S(2)}) collective-permute-start(bf16[128,768]{1,0:T(8,128)(2,1)S(1)} %get-tuple-element.200), channel_id=1, source_target_pairs={{0,1},{1,2},{2,3},{3,0},{4,5},{5,6},{6,7},{7,4},{8,9},{9,10},{10,1... | collective-permute-start | bytes 589832 | tf_op jit(solution)/shard_map/ppermute | solution.py:1067
  71.6 14.2 %collective-permute-start.12 = (bf16[128,768]{1,0:T(8,128)(2,1)S(1)}, bf16[128,768]{1,0:T(8,128)(2,1)S(1)}, u32[]{:S(2)}, u32[]{:S(2)}) collective-permute-start(bf16[128,768]{1,0:T(8,128)(2,1)S(1)} %get-tuple-element.201), channel_id=1, source_target_pairs={{0,2},{1,3},{2,0},{3,1},{4,6},{5,7},{6,4},{7,5},{8,10},{9,11},{10,... | collective-permute-start | bytes 589832 | tf_op jit(solution)/shard_map/ppermute | solution.py:1067
  73.1 19.5 %collective-permute-start.14 = (bf16[192,768]{1,0:T(8,128)(2,1)S(1)}, bf16[192,768]{1,0:T(8,128)(2,1)S(1)}, u32[]{:S(2)}, u32[]{:S(2)}) collective-permute-start(bf16[192,768]{1,0:T(8,128)(2,1)S(1)} %get-tuple-element.209.refs_0_), channel_id=1, source_target_pairs={{0,8},{4,12},{8,0},{12,4},{16,24},{20,28},{24,16},{28,20},{1,9},{5... | collective-permute-start | bytes 884744 | tf_op jit(solution)/shard_map/ppermute | solution.py:224
  74.6 21.2 %collective-permute-start.15 = (bf16[192,768]{1,0:T(8,128)(2,1)S(1)}, bf16[192,768]{1,0:T(8,128)(2,1)S(1)}, u32[]{:S(2)}, u32[]{:S(2)}) collective-permute-start(bf16[192,768]{1,0:T(8,128)(2,1)S(1)} %get-tuple-element.210.refs_1_), channel_id=1, source_target_pairs={{0,16},{4,20},{8,24},{12,28},{16,0},{20,4},{24,8},{28,12},{1,17},{... | collective-permute-start | bytes 884744 | tf_op jit(solution)/shard_map/ppermute | solution.py:224
  76.2 11.2 %collective-permute-start.13 = (bf16[128,768]{1,0:T(8,128)(2,1)S(1)}, bf16[128,768]{1,0:T(8,128)(2,1)S(1)}, u32[]{:S(2)}, u32[]{:S(2)}) collective-permute-start(bf16[128,768]{1,0:T(8,128)(2,1)S(1)} %get-tuple-element.202), channel_id=1, source_target_pairs={{0,3},{1,0},{2,1},{3,2},{4,7},{5,4},{6,5},{7,6},{8,11},{9,8},{10,9... | collective-permute-start | bytes 589832 | tf_op jit(solution)/shard_map/ppermute | solution.py:1067
  79.1 17.3 %collective-permute-start.16 = (bf16[192,768]{1,0:T(8,128)(2,1)S(1)}, bf16[192,768]{1,0:T(8,128)(2,1)S(1)}, u32[]{:S(2)}, u32[]{:S(2)}) collective-permute-start(bf16[192,768]{1,0:T(8,128)(2,1)S(1)} %get-tuple-element.211.refs_2_), channel_id=1, source_target_pairs={{0,8},{4,12},{8,0},{12,4},{16,24},{20,28},{24,16},{28,20},{1,9},{5... | collective-permute-start | bytes 884744 | tf_op jit(solution)/shard_map/ppermute | solution.py:224
  85.9 10.6 %collective-permute-start.17 = (bf16[192,768]{1,0:T(8,128)(2,1)S(1)}, bf16[192,768]{1,0:T(8,128)(2,1)S(1)}, u32[]{:S(2)}, u32[]{:S(2)}) collective-permute-start(bf16[192,768]{1,0:T(8,128)(2,1)S(1)} %get-tuple-element.212.refs_3_), channel_id=1, source_target_pairs={{0,16},{4,20},{8,24},{12,28},{16,0},{20,4},{24,8},{28,12},{1,17},{... | collective-permute-start | bytes 884744 | tf_op jit(solution)/shard_map/ppermute | solution.py:224
  87.8 17.8 %collective-permute-start.18 = (bf16[128,768]{1,0:T(8,128)(2,1)S(1)}, bf16[128,768]{1,0:T(8,128)(2,1)S(1)}, u32[]{:S(2)}, u32[]{:S(2)}) collective-permute-start(bf16[128,768]{1,0:T(8,128)(2,1)S(1)} %get-tuple-element.216), channel_id=1, source_target_pairs={{0,2},{1,3},{2,0},{3,1},{4,6},{5,7},{6,4},{7,5},{8,10},{9,11},{10,... | collective-permute-start | bytes 589832 | tf_op jit(solution)/shard_map/ppermute | solution.py:1067
  92.6 13.0 %collective-permute-start.19 = (bf16[128,768]{1,0:T(8,128)(2,1)S(1)}, bf16[128,768]{1,0:T(8,128)(2,1)S(1)}, u32[]{:S(2)}, u32[]{:S(2)}) collective-permute-start(bf16[128,768]{1,0:T(8,128)(2,1)S(1)} %get-tuple-element.217), channel_id=1, source_target_pairs={{0,1},{1,2},{2,3},{3,0},{4,5},{5,6},{6,7},{7,4},{8,9},{9,10},{10,1... | collective-permute-start | bytes 589832 | tf_op jit(solution)/shard_map/ppermute | solution.py:1067
  95.9 10.4 %collective-permute-start.20 = (bf16[128,768]{1,0:T(8,128)(2,1)S(1)}, bf16[128,768]{1,0:T(8,128)(2,1)S(1)}, u32[]{:S(2)}, u32[]{:S(2)}) collective-permute-start(bf16[128,768]{1,0:T(8,128)(2,1)S(1)} %get-tuple-element.218), channel_id=1, source_target_pairs={{0,3},{1,0},{2,1},{3,2},{4,7},{5,4},{6,5},{7,6},{8,11},{9,8},{10,9... | collective-permute-start | bytes 589832 | tf_op jit(solution)/shard_map/ppermute | solution.py:1067
  96.7 18.7 %collective-permute-start.21 = (bf16[384,768]{1,0:T(8,128)(2,1)S(1)}, bf16[384,768]{1,0:T(8,128)(2,1)S(1)}, u32[]{:S(2)}, u32[]{:S(2)}) collective-permute-start(bf16[384,768]{1,0:T(8,128)(2,1)S(1)} %get-tuple-element.227.own_a), channel_id=1, source_target_pairs={{0,16},{4,20},{8,24},{12,28},{16,0},{20,4},{24,8},{28,12},{1,17},{... | collective-permute-start | bytes 1769480 | tf_op jit(solution)/shard_map/ppermute | solution.py:224
  97.3 18.1 %collective-permute-start.22 = (bf16[384,768]{1,0:T(8,128)(2,1)S(1)}, bf16[384,768]{1,0:T(8,128)(2,1)S(1)}, u32[]{:S(2)}, u32[]{:S(2)}) collective-permute-start(bf16[384,768]{1,0:T(8,128)(2,1)S(1)} %get-tuple-element.228.own_b), channel_id=1, source_target_pairs={{0,8},{4,12},{8,0},{12,4},{16,24},{20,28},{24,16},{28,20},{1,9},{5... | collective-permute-start | bytes 1769480 | tf_op jit(solution)/shard_map/ppermute | solution.py:224
  115.3 2.1 %collective-permute-start.23 = (bf16[400,768]{1,0:T(8,128)(2,1)S(1)}, bf16[400,768]{1,0:T(8,128)(2,1)S(1)}, u32[]{:S(2)}, u32[]{:S(2)}) collective-permute-start(bf16[400,768]{1,0:T(8,128)(2,1)S(1)} %get-tuple-element.230), channel_id=1, source_target_pairs={{0,4},{4,0},{8,12},{12,8},{16,20},{20,16},{24,28},{28,24},{1,5},{5... | collective-permute-start | bytes 1843208 | tf_op jit(solution)/shard_map/ppermute | solution.py:224
  115.7 13.6 %collective-permute-start.26 = (bf16[768,768]{1,0:T(8,128)(2,1)S(1)}, bf16[768,768]{1,0:T(8,128)(2,1)S(1)}, u32[]{:S(2)}, u32[]{:S(2)}) collective-permute-start(bf16[768,768]{1,0:T(8,128)(2,1)S(1)} %fold_feed_last.1.mine), channel_id=1, source_target_pairs={{0,4},{4,0},{8,12},{12,8},{16,20},{20,16},{24,28},{28,24},{1,5},{5... | collective-permute-start | bytes 3538952 | tf_op jit(solution)/shard_map/ppermute | solution.py:224
  117.5 9.6 %collective-permute-start.24 = (bf16[208,768]{1,0:T(8,128)(2,1)S(1)}, bf16[208,768]{1,0:T(8,128)(2,1)S(1)}, u32[]{:S(2)}, u32[]{:S(2)}) collective-permute-start(bf16[208,768]{1,0:T(8,128)(2,1)S(1)} %get-tuple-element.239.own_a), channel_id=1, source_target_pairs={{0,8},{4,12},{8,0},{12,4},{16,24},{20,28},{24,16},{28,20},{1,9},{5... | collective-permute-start | bytes 958472 | tf_op jit(solution)/shard_map/ppermute | solution.py:224
  118.2 8.8 %collective-permute-start.25 = (bf16[192,768]{1,0:T(8,128)(2,1)S(1)}, bf16[192,768]{1,0:T(8,128)(2,1)S(1)}, u32[]{:S(2)}, u32[]{:S(2)}) collective-permute-start(bf16[192,768]{1,0:T(8,128)(2,1)S(1)} %get-tuple-element.240.own_b), channel_id=1, source_target_pairs={{0,16},{4,20},{8,24},{12,28},{16,0},{20,4},{24,8},{28,12},{1,17},{... | collective-permute-start | bytes 884744 | tf_op jit(solution)/shard_map/ppermute | solution.py:224
  119.4 9.8 %copy-start.5 = (f32[2,768]{1,0:T(2,128)S(1)}, f32[2,768]{1,0:T(2,128)}, u32[]{:S(2)}) copy-start(f32[2,768]{1,0:T(2,128)} %wide_old.1) | copy-start | bytes 18436
  127.2 11.2 %copy-start.2 = (f32[4,2,768]{2,1,0:T(2,128)S(1)}, f32[4,2,768]{2,1,0:T(2,128)}, u32[]{:S(2)}) copy-start(f32[4,2,768]{2,1,0:T(2,128)} %stats.3) | copy-start | bytes 73732
  127.4 8.8 %collective-permute-start.27 = (bf16[208,768]{1,0:T(8,128)(2,1)S(1)}, bf16[208,768]{1,0:T(8,128)(2,1)S(1)}, u32[]{:S(2)}, u32[]{:S(2)}) collective-permute-start(bf16[208,768]{1,0:T(8,128)(2,1)S(1)} %get-tuple-element.246.own_a), channel_id=1, source_target_pairs={{0,16},{4,20},{8,24},{12,28},{16,0},{20,4},{24,8},{28,12},{1,17},{... | collective-permute-start | bytes 958472 | tf_op jit(solution)/shard_map/ppermute | solution.py:224
  128.4 7.6 %collective-permute-start.28 = (bf16[192,768]{1,0:T(8,128)(2,1)S(1)}, bf16[192,768]{1,0:T(8,128)(2,1)S(1)}, u32[]{:S(2)}, u32[]{:S(2)}) collective-permute-start(bf16[192,768]{1,0:T(8,128)(2,1)S(1)} %get-tuple-element.247.own_b), channel_id=1, source_target_pairs={{0,8},{4,12},{8,0},{12,4},{16,24},{20,28},{24,16},{28,20},{1,9},{5... | collective-permute-start | bytes 884744 | tf_op jit(solution)/shard_map/ppermute | solution.py:224
  136.2 13.5 %copy-start.3 = (f32[4,768]{1,0:T(4,128)S(1)}, f32[4,768]{1,0:T(4,128)}, u32[]{:S(2)}) copy-start(f32[4,768]{1,0:T(4,128)} %vec_moment.1) | copy-start | bytes 36868
  136.2 13.5 %copy-start.4 = (f32[2,768]{1,0:T(2,128)S(1)}, f32[2,768]{1,0:T(2,128)}, u32[]{:S(2)}) copy-start(f32[2,768]{1,0:T(2,128)} %narrow_old.1) | copy-start | bytes 18436
  136.3 2.1 %collective-permute-start.29 = (bf16[384,768]{1,0:T(8,128)(2,1)S(1)}, bf16[384,768]{1,0:T(8,128)(2,1)S(1)}, u32[]{:S(2)}, u32[]{:S(2)}) collective-permute-start(bf16[384,768]{1,0:T(8,128)(2,1)S(1)} %get-tuple-element.249.even), channel_id=1, source_target_pairs={{0,4},{4,0},{8,12},{12,8},{16,20},{20,16},{24,28},{28,24},{1,5},{5... | collective-permute-start | bytes 1769480 | tf_op jit(solution)/shard_map/ppermute | solution.py:224
  140.1 7.5 %collective-permute-start.32 = (bf16[32,768]{1,0:T(8,128)(2,1)S(1)}, bf16[32,768]{1,0:T(8,128)(2,1)S(1)}, u32[]{:S(2)}, u32[]{:S(2)}) collective-permute-start(bf16[32,768]{1,0:T(8,128)(2,1)S(1)} %get-tuple-element.263.share), channel_id=1, source_target_pairs={{0,3},{1,2},{2,1},{3,0},{4,7},{5,6},{6,5},{7,4},{8,11},{9,10},{10,... | collective-permute-start | bytes 147464 | tf_op jit(solution)/shard_map/ppermute | solution.py:1067
  143.8 5.0 %collective-permute-start.31 = (bf16[32,768]{1,0:T(8,128)(2,1)S(1)}, bf16[32,768]{1,0:T(8,128)(2,1)S(1)}, u32[]{:S(2)}, u32[]{:S(2)}) collective-permute-start(bf16[32,768]{1,0:T(8,128)(2,1)S(1)} %get-tuple-element.263.share), channel_id=1, source_target_pairs={{0,2},{1,3},{2,0},{3,1},{4,6},{5,7},{6,4},{7,5},{8,10},{9,11},{10,... | collective-permute-start | bytes 147464 | tf_op jit(solution)/shard_map/ppermute | solution.py:1067
  145.6 4.1 %collective-permute-start.30 = (bf16[32,768]{1,0:T(8,128)(2,1)S(1)}, bf16[32,768]{1,0:T(8,128)(2,1)S(1)}, u32[]{:S(2)}, u32[]{:S(2)}) collective-permute-start(bf16[32,768]{1,0:T(8,128)(2,1)S(1)} %get-tuple-element.263.share), channel_id=1, source_target_pairs={{0,1},{1,0},{2,3},{3,2},{4,5},{5,4},{6,7},{7,6},{8,9},{9,8},{10,11... | collective-permute-start | bytes 147464 | tf_op jit(solution)/shard_map/ppermute | solution.py:1067
